TPU v7x, 32 devices: a whole 2x2x4 slice. The times are simulated.
32 devices in a mesh: nodes: 8 (over z, x), grid: 4 (over y, core).
Axes of the slice: x: 2, y: 2, z: 4, core: 2. Of those that a mesh axis runs over, the one named last changes fastest.
Arguments:
- block: float32 [256, 65536], P('grid', 'nodes')
- inv_sqrt_mass: float32 [65536], P('nodes'), may hold values from 0.6 to 1.6
- potential: float32 [65536], P('nodes'), may hold values from -2 to 1
- elem_scale: float32 [1024], P('nodes'), may hold values from 0.5 to 2
- connectivity: int32 [1024, 125], P('nodes'), may hold values from 0 to 10239, as said below
- elem_matrix: float32 [125, 125], replicated, as said below
Outputs:
- filtered_cyclic: float32 [256, 65536], P('grid', 'nodes')
- intersection: float32 [256, 256], P(None, 'grid')
Inputs may be any that keep to these rules, and one draw needn't show every extreme that they name: `connectivity`: each row is an element of partition p = row // 128; its entries number the partition's 8192 own nodes from 0, then from 8192 the first 2048 nodes of the next partition. Element j of a partition uses nodes j * 64 to j * 64 + 2111; entries may repeat within an element. `elem_matrix`: Symmetric, with diagonal entries about 3 plus a full off-diagonal part.
All inputs are finite; a program needn't handle non-finite values.
Results may differ from a plain program's by a relative error of at most 0.0003.
Values sent between devices are 32-bit elements; how exact they have to be, the bound alone decides.
A program may use at most 64 MiB of HBM per device.

v0:
```python
import jax
import jax.numpy as jnp
from jax import lax
from jax.sharding import PartitionSpec as P

RIM = 2048
NB = 128


def from_behind(value, axis, steps):
    count = lax.axis_size(axis)
    leading, last = (max(0, -steps), min(count, count - steps))
    return lax.ppermute(value, axis, [(source, source + steps) for source in range(leading, last)])


def apply_operator(field, inv_sqrt_mass, potential, elem_scale, conn_t, elem_matrix):
    owned = field.shape[1]
    scaled = inv_sqrt_mass[None, :] * field
    upper = from_behind(scaled[:, :RIM], "nodes", -1)
    wide = jnp.concatenate([scaled, upper], axis=1)
    picked = wide[:, conn_t]
    local = jnp.einsum("ab,sbe->sae", elem_matrix, picked, precision=lax.Precision.HIGHEST)
    local = local * elem_scale[None, None, :]
    summed = jnp.zeros(wide.shape, jnp.float32).at[:, conn_t].add(local)
    lower = from_behind(summed[:, owned:], "nodes", 1)
    assembled = summed[:, :owned] + jnp.pad(lower, ((0, 0), (0, owned - RIM)))
    return inv_sqrt_mass[None, :] * assembled + potential[None, :] * field


def shards(block, inv_sqrt_mass, potential, elem_scale, connectivity, elem_matrix):
    conn_t = connectivity.T
    lowest, cut, top = (-2.0, 4.0, 32.0)
    half = (top - cut) / 2.0
    centre = (top + cut) / 2.0
    sigma = half / (lowest - centre)
    sigma_two = 1.0 / (2.0 / sigma - sigma)
    image = apply_operator(block, inv_sqrt_mass, potential, elem_scale, conn_t, elem_matrix)
    first = sigma / half * (image - centre * block)
    image_two = apply_operator(first, inv_sqrt_mass, potential, elem_scale, conn_t, elem_matrix)
    filtered = 2.0 * (sigma_two / half) * (image_two - centre * first) - sigma * sigma_two * block
    states, owned = filtered.shape
    parts = lax.axis_size("nodes")
    columns = lax.axis_size("grid")
    blocks = owned // (parts * NB)
    shaped = filtered.reshape(columns, states // columns, blocks, parts, NB).transpose(
        0, 1, 3, 2, 4
    )
    moved = lax.all_to_all(
        lax.all_to_all(shaped, "nodes", split_axis=2, concat_axis=2, tiled=True),
        "grid",
        split_axis=0,
        concat_axis=0,
        tiled=True,
    )
    cyclic = moved.reshape(states, owned)
    weight = 1.0 / (owned * parts)
    partial_value = (
        jnp.dot(
            lax.all_gather(cyclic, "grid", axis=0, tiled=True),
            cyclic.T,
            precision=lax.Precision.HIGHEST,
        )
        * weight
    )
    intersection = lax.psum(partial_value, "nodes")
    return (cyclic, intersection)


def solution(mesh):
    placed = (P("grid", "nodes"), P("nodes"), P("nodes"), P("nodes"), P("nodes", None), P())
    return jax.shard_map(
        shards,
        mesh=mesh,
        in_specs=placed,
        out_specs=(P("grid", "nodes"), P(None, "grid")),
        check_vma=False,
    )
```

profile of v0, /device:TPU:0, one launch (start us, length us, event | category | flops | bytes accessed | tf_op | source)
XLA Modules:
  0.0 614.5 jit_solution(3516712380021721600)
XLA Ops:
  7.2 0.0 copy-start
  7.2 0.0 copy-start.6
  7.2 0.0 all-gather.2.cloned.1.call-start
  7.2 1.8 broadcast_multiply_fusion.1
  9.1 1.3 collective-permute-start
  10.4 0.0 copy-done.6
  10.4 0.1 copy.85
  10.5 15.3 %collective-permute-done = f32[64,2048]{1,0:T(8,128)S(1)} collective-permute-done((f32[64,2048]{1,0:T(8,128)S(1)}, f32[64,2048]{1,0:T(8,128)S(1)}, u32[]{:S(2)}, u32[]{:S(2)}) %collective-permute-start) | collective-permute-done | bytes 524320 | tf_op jit(solution)/shard_map/ppermute | solution.py:13
  25.8 1.7 pad_maximum_fusion
  27.5 5.3 copy.86
  32.8 32.8 %gather_fusion = f32[16000,64]{1,0:T(8,128)} fusion(f32[64,10240]{0,1:T(8,128)} %copy.86, s32[16384]{0:T(1024)S(1)} %pad_clamp_fusion), kind=kCustom, calls=%fused_computation | custom fusion | bytes 8256000 | tf_op jit(solution)/shard_map/gather | solution.py:21
  65.6 0.0 copy-start.7
  65.6 9.0 %copy.87 = f32[125,128,64]{0,1,2:T(8,128)} copy(f32[125,128,64]{2,1,0:T(8,128)} %bitcast.38) | data formatting | bytes 8192000 | tf_op jit(solution)/shard_map/gather | solution.py:21
  74.6 0.0 copy-done
  74.6 0.0 copy-done.7
  74.6 6.5 %multiply_bitcast_fusion.1 = f32[125,128,64]{0,1,2:T(8,128)} fusion(f32[125,128,64]{0,1,2:T(8,128)} %copy.87, f32[128]{0:T(128)S(1)} %copy-done.7, f32[125,125]{1,0:T(8,128)S(1)} %copy-done), kind=kOutput, calls=%fused_computation.9 | convolution fusion | flops 1537024000 | bytes 8255012 | tf_op jit(solution)/shard_map/ab,sbe->sae/dot_general | solution.py:22
  81.1 9.3 %copy.101 = f32[125,128,64]{2,1,0:T(8,128)} copy(f32[125,128,64]{0,1,2:T(8,128)} %multiply_bitcast_fusion.1) | data formatting | bytes 8192000 | tf_op jit(solution)/shard_map/mul | solution.py:23
  90.4 90.6 %scatter_custom_fusion = f32[64,10240]{0,1:T(8,128)} fusion(s32[16000]{0:T(1024)S(1)} %fusion.12, f32[16000,64]{1,0:T(8,128)} %bitcast.41, f32[]{:T(128)} %constant.2.clone.1), kind=kCustom, calls=%fused_computation.14 | custom fusion | flops 1024000 | bytes 2621952 | tf_op jit(solution)/shard_map/scatter-add | solution.py:24
  181.1 0.0 slice-start.1
  181.1 0.0 copy-start.4
  181.1 1.2 slice-done.1
  182.3 1.1 copy.91
  183.4 4.6 collective-permute-start.1
  188.0 0.0 copy-done.4
  188.0 4.4 slice.29
  192.4 0.0 copy-start.5
  192.4 2.8 copy.105
  195.2 3.3 collective-permute-done.1
  198.5 0.0 copy-done.5
  198.5 0.0 copy-start.2
  198.5 2.2 broadcast_multiply_fusion
  200.8 0.0 copy-done.2
  200.8 1.5 collective-permute-start.2
  202.3 12.9 %collective-permute-done.2 = f32[64,2048]{1,0:T(8,128)S(1)} collective-permute-done((f32[64,2048]{1,0:T(8,128)S(1)}, f32[64,2048]{1,0:T(8,128)S(1)}, u32[]{:S(2)}, u32[]{:S(2)}) %collective-permute-start.2) | collective-permute-done | bytes 524320 | tf_op jit(solution)/shard_map/ppermute | solution.py:13
  215.2 1.6 pad_maximum_fusion.1
  216.9 5.3 copy.92
  222.1 32.7 %gather_fusion.1 = f32[16000,64]{1,0:T(8,128)} fusion(f32[64,10240]{0,1:T(8,128)} %copy.92, s32[16384]{0:T(1024)S(1)} %pad_clamp_fusion), kind=kCustom, calls=%fused_computation.1 | custom fusion | bytes 8256000 | tf_op jit(solution)/shard_map/gather | solution.py:21
  254.9 9.0 %copy.93 = f32[125,128,64]{0,1,2:T(8,128)} copy(f32[125,128,64]{2,1,0:T(8,128)} %bitcast.37) | data formatting | bytes 8192000 | tf_op jit(solution)/shard_map/gather | solution.py:21
  263.8 6.6 %multiply_bitcast_fusion = f32[125,128,64]{0,1,2:T(8,128)} fusion(f32[125,128,64]{0,1,2:T(8,128)} %copy.93, f32[128]{0:T(128)S(1)} %copy-done.7, f32[125,125]{1,0:T(8,128)S(1)} %copy-done), kind=kOutput, calls=%fused_computation.8 | convolution fusion | flops 1537024000 | bytes 8255012 | tf_op jit(solution)/shard_map/ab,sbe->sae/dot_general | solution.py:22
  270.4 9.2 %copy.102 = f32[125,128,64]{2,1,0:T(8,128)} copy(f32[125,128,64]{0,1,2:T(8,128)} %multiply_bitcast_fusion) | data formatting | bytes 8192000 | tf_op jit(solution)/shard_map/mul | solution.py:23
  279.7 90.6 %scatter_custom_fusion.1 = f32[64,10240]{0,1:T(8,128)} fusion(s32[16000]{0:T(1024)S(1)} %fusion.12, f32[16000,64]{1,0:T(8,128)} %bitcast.40, f32[]{:T(128)} %constant.2.clone.1), kind=kCustom, calls=%fused_computation.12 | custom fusion | flops 1024000 | bytes 2621952 | tf_op jit(solution)/shard_map/scatter-add | solution.py:24
  370.3 1.2 slice-done
  371.5 1.1 copy.97
  372.6 4.6 collective-permute-start.3
  377.2 4.5 slice.32
  381.7 3.8 copy.106
  385.5 0.4 collective-permute-done.3
  385.9 0.0 copy-done.3
  385.9 3.1 subtract_bitcast_fusion
  389.0 0.4 copy.107
  389.4 0.4 copy.98
  389.8 50.2 %all_to_all.10 = f32[4,16,8,8,128]{4,3,1,0,2:T(8,128)S(1)} all-to-all(f32[4,16,8,8,128]{4,3,1,0,2:T(8,128)S(1)} %copy.98), channel_id=1, replica_groups=mesh['nodes'=8,'grid'=4] {'nodes'}, dimensions={2} | all-to-all | bytes 4194304 | tf_op jit(solution)/shard_map/all_to_all | solution.py:49
  440.0 0.2 copy.99
  440.2 28.3 %all_to_all.11 = f32[4,16,8,8,128]{4,3,1,2,0:T(8,128)S(1)} all-to-all(f32[4,16,8,8,128]{4,3,1,2,0:T(8,128)S(1)} %copy.99), channel_id=1, replica_groups=mesh['nodes'=8,'grid'=4] {'grid'}, dimensions={0} | all-to-all | bytes 4194304 | tf_op jit(solution)/shard_map/all_to_all | solution.py:48
  468.5 0.3 copy.100
  468.8 1.5 reshape.14
  470.3 0.0 all-gather.2.cloned.1.call-update
  470.3 0.0 all-reduce.4.cloned.1.call-start
  470.4 56.5 %all-gather.2.cloned.1.call-done = f32[256,8192]{1,0:T(8,128)} async-done(((f32[64,8192]{1,0:T(8,128)}), f32[256,8192]{1,0:T(8,128)}) %all-gather.2.cloned.1.call-update) | async-done | bytes 8388624 | tf_op jit(solution)/shard_map/all_gather | solution.py:59
  526.9 0.0 copy-done.1
  526.9 10.7 %convolution_multiply_fusion = f32[256,64]{0,1:T(8,128)} fusion(f32[256,8192]{1,0:T(8,128)} %all-gather.2.cloned.1.call-done, f32[64,8192]{1,0:T(8,128)S(1)} %copy-done.1), kind=kOutput, calls=%fused_computation.18 | convolution fusion | flops 1610629120 | bytes 10551296 | tf_op jit(solution)/shard_map/dot_general | solution.py:58
  537.6 0.0 all-reduce.4.cloned.1.call-update
  537.6 68.6 %all-reduce.4.cloned.1.call-done = f32[256,64]{0,1:T(8,128)} async-done(((f32[256,64]{0,1:T(8,128)}), f32[256,64]{0,1:T(8,128)}) %all-reduce.4.cloned.1.call-update) | async-done | bytes 65552 | tf_op jit(solution)/shard_map/psum | solution.py:65
  606.2 1.5 copy.109
  (9 shorter events, 0.1 us)
Async XLA Ops:
  7.2 67.4 %copy-start = (f32[125,125]{1,0:T(8,128)S(1)}, f32[125,125]{1,0:T(8,128)}, u32[]{:S(2)}) copy-start(f32[125,125]{1,0:T(8,128)} %param.11) | copy-start | bytes 187504
  7.2 3.2 copy-start.6
  7.2 519.7 %all-gather.2.cloned.1.call-start = ((), (), s32[]{:S(2)}) async-start(), calls=%async_computation.2 | async-start | bytes 10485760 | tf_op jit(solution)/shard_map/all_gather | solution.py:59
  9.1 16.8 %collective-permute-start = (f32[64,2048]{1,0:T(8,128)S(1)}, f32[64,2048]{1,0:T(8,128)S(1)}, u32[]{:S(2)}, u32[]{:S(2)}) collective-permute-start(f32[64,2048]{1,0:T(8,128)S(1)} %slice.28), channel_id=1, source_target_pairs={{4,0},{8,4},{12,8},{16,12},{20,16},{24,20},{28,24},{5,1},{9,5},{13... | collective-permute-start | bytes 1572872 | tf_op jit(solution)/shard_map/ppermute | solution.py:13
  65.6 9.0 %copy-start.7 = (f32[128]{0:T(128)S(1)}, f32[128]{0:T(128)}, u32[]{:S(2)}) copy-start(f32[128]{0:T(128)} %param.9) | copy-start | bytes 1540
  181.1 1.2 slice-start.1
  181.1 6.9 %copy-start.4 = (f32[8192]{0:T(1024)S(1)}, f32[8192]{0:T(1024)}, u32[]{:S(2)}) copy-start(f32[8192]{0:T(1024)} %param.7) | copy-start | bytes 98308
  183.4 15.1 %collective-permute-start.1 = (f32[64,2048]{1,0:T(8,128)}, f32[64,2048]{1,0:T(8,128)S(1)}, u32[]{:S(2)}, u32[]{:S(2)}) collective-permute-start(f32[64,2048]{1,0:T(8,128)} %copy.91), channel_id=1, source_target_pairs={{0,4},{4,8},{8,12},{12,16},{16,20},{20,24},{24,28},{1,5},{5,9},{9,... | collective-permute-start | bytes 1572872 | tf_op jit(solution)/shard_map/ppermute | solution.py:13
  192.4 6.2 %copy-start.5 = (f32[8192]{0:T(1024)S(1)}, f32[8192]{0:T(1024)}, u32[]{:S(2)}) copy-start(f32[8192]{0:T(1024)} %param.8) | copy-start | bytes 98308
  198.5 2.2 copy-start.2
  200.8 14.4 %collective-permute-start.2 = (f32[64,2048]{1,0:T(8,128)S(1)}, f32[64,2048]{1,0:T(8,128)S(1)}, u32[]{:S(2)}, u32[]{:S(2)}) collective-permute-start(f32[64,2048]{1,0:T(8,128)S(1)} %slice.31), channel_id=1, source_target_pairs={{4,0},{8,4},{12,8},{16,12},{20,16},{24,20},{28,24},{5,1},{9,5},{13... | collective-permute-start | bytes 1572872 | tf_op jit(solution)/shard_map/ppermute | solution.py:13
  370.3 1.2 slice-start
  372.6 13.3 %collective-permute-start.3 = (f32[64,2048]{1,0:T(8,128)}, f32[64,2048]{1,0:T(8,128)S(1)}, u32[]{:S(2)}, u32[]{:S(2)}) collective-permute-start(f32[64,2048]{1,0:T(8,128)} %copy.97), channel_id=1, source_target_pairs={{0,4},{4,8},{8,12},{12,16},{16,20},{20,24},{24,28},{1,5},{5,9},{9,... | collective-permute-start | bytes 1572872 | tf_op jit(solution)/shard_map/ppermute | solution.py:13
  381.6 4.2 copy-start.3
  470.3 56.6 %copy-start.1 = (f32[64,8192]{1,0:T(8,128)S(1)}, f32[64,8192]{1,0:T(8,128)}, u32[]{:S(2)}) copy-start(f32[64,8192]{1,0:T(8,128)} %reshape.14) | copy-start | bytes 6291460
  470.3 135.9 %all-reduce.4.cloned.1.call-start = ((), (), s32[]{:S(2)}) async-start(), calls=%async_computation.3 | async-start | bytes 131072 | tf_op jit(solution)/shard_map/psum | solution.py:65
Sparse Core Ops, SparseCore 0:
  470.5 56.3 all-gather.1
  537.7 68.4 all-reduce.3
where the time goes:
time: 616 us; the launch traced here: 615 us
  other arithmetic  192 us (31%)
  waiting for transfers between devices  157 us (25%)
  local copies, waits for them, and re-layouts  137 us (22%)
  blocking collectives  78.4 us (13%)
  matrix products  23.8 us (4%)
  between operations  14.2 us (2%)
  starting transfers between devices  12 us (2%)
    scatter-add x2, other arithmetic, apply_operator(): summed = jnp.zeros(wide.shape, jnp.float32).at[:, conn_t].add(local)  181 us
    gather x4, local copies, waits for them, and re-layouts, apply_operator(): picked = wide[:, conn_t]  83.4 us
    psum x1, waiting for transfers between devices, shards(): intersection = lax.psum(partial_value, 'nodes')  68.6 us
    all_gather x1, waiting for transfers between devices, shards(): lax.all_gather(cyclic, 'grid', axis=0, tiled=True)  56.5 us
    all_to_all x1, blocking collectives, shards(): lax.all_to_all(shaped, 'nodes', split_axis=2, concat_axis=2, tiled=True)  50.2 us
    ppermute x4, waiting for transfers between devices, from_behind(): lax.ppermute(value, axis, [(source, source + steps) for source in range(l...  31.9 us
    all_to_all x1, blocking collectives, shards(): lax.all_to_all(lax.all_to_all(shaped, 'nodes', split_axis=2, concat_axis=...  28.3 us
    mul x2, local copies, waits for them, and re-layouts, apply_operator(): local = local * elem_scale[None, None, :]  18.6 us
  transfers between devices with their start and end apart: 6, of which 6 were waited for; matrix products, arithmetic and copies ran while one was open for 3% of the time, Pallas kernels for 0%

commit v1 on v0

v1 whole, which is shorter than its diff:
```python
import functools
import jax
import jax.numpy as jnp
from jax import lax
from jax.experimental import pallas as pl
from jax.experimental.pallas import tpu as pltpu
from jax.sharding import PartitionSpec as P

RIM = 2048
NB = 128
SB = 16
GROUP = 4
CHAINS = 4
BOTH = ("nodes", "grid")


def split(value):
    high = value.astype(jnp.bfloat16)
    return high, (value - high.astype(jnp.float32)).astype(jnp.bfloat16)


def dot(a, b):
    return jnp.dot(a, b, preferred_element_type=jnp.float32)


def operator_kernel(npe, index_ref, scale_ref, matrix_ref, wide_ref, out_ref, picked, local, *sums):
    groups = scale_ref.shape[0] // GROUP
    m_high, m_low = split(matrix_ref[...])
    picked[...] = jnp.zeros_like(picked)
    for total in sums:
        total[...] = jnp.zeros_like(total)

    def gather(first, i, m):
        node = index_ref[(first + m) * npe + i]
        picked[i : i + 1, m * 128 : (m + 1) * 128] = wide_ref[pl.ds(node, 1), :]

    for i in range(npe):
        for m in range(GROUP):
            gather(0, i, m)

    @pl.loop(0, groups)
    def _(g):
        here = g * GROUP
        later = jnp.minimum(g + 1, groups - 1) * GROUP
        high, low = split(picked[...])
        product = dot(m_high, high) + (dot(m_high, low) + dot(m_low, high))
        for m in range(GROUP):
            local[:, m * 128 : (m + 1) * 128] = (
                product[:, m * 128 : (m + 1) * 128] * scale_ref[here + m]
            )
        for i in range(npe):
            for m in range(GROUP):
                total = sums[(i * GROUP + m) % len(sums)]
                node = index_ref[(here + m) * npe + i]
                total[pl.ds(node, 1), :] += local[i : i + 1, m * 128 : (m + 1) * 128]
                gather(later, i, m)

    value = sums[0][...]
    for total in sums[1:]:
        value = value + total[...]
    out_ref[...] = value


def element_sums(wide, index, scale, matrix):
    count, npe = index.shape
    vmem = pl.BlockSpec(memory_space=pltpu.VMEM)
    smem = pl.BlockSpec(memory_space=pltpu.SMEM)
    rows = matrix.shape[0]
    return pl.pallas_call(
        functools.partial(operator_kernel, npe),
        out_shape=jax.ShapeDtypeStruct(wide.shape, jnp.float32),
        in_specs=[smem, smem, vmem, vmem],
        out_specs=vmem,
        scratch_shapes=[pltpu.VMEM((rows, GROUP * 128), jnp.float32)] * 2
        + [pltpu.VMEM(wide.shape, jnp.float32)] * CHAINS,
        compiler_params=pltpu.CompilerParams(vmem_limit_bytes=44 * 1024 * 1024),
    )(index.reshape(-1), scale, matrix, wide)


def shards(block, inv_sqrt_mass, potential, elem_scale, connectivity, elem_matrix):
    lowest, cut, top = (-2.0, 4.0, 32.0)
    half = (top - cut) / 2.0
    centre = (top + cut) / 2.0
    sigma = half / (lowest - centre)
    sigma_two = 1.0 / (2.0 / sigma - sigma)
    parts = lax.axis_size("nodes")
    columns = lax.axis_size("grid")
    states, owned = block.shape
    mine = owned // 2
    core = lax.axis_index("grid") % 2
    elements = connectivity.shape[0] // 2

    ups, downs = [], []
    for y in range(columns // 2):
        for t in range(2 * parts - 1):
            a = (t // 2) * columns + 2 * y + t % 2
            b = ((t + 1) // 2) * columns + 2 * y + (t + 1) % 2
            ups.append((a, b))
            downs.append((b, a))

    index = lax.dynamic_slice_in_dim(connectivity, core * elements, elements, 0) - core * mine
    scale = lax.dynamic_slice_in_dim(elem_scale, core * elements, elements, 0)
    mass = lax.dynamic_slice_in_dim(inv_sqrt_mass, core * mine, mine, 0)[:, None]
    pot = lax.dynamic_slice_in_dim(potential, core * mine, mine, 0)[:, None]
    pad = -elem_matrix.shape[0] % 128
    matrix = jnp.pad(elem_matrix, ((0, pad), (0, pad)))

    away = lax.dynamic_slice_in_dim(block, (1 - core) * mine, mine, 1)
    kept = lax.dynamic_slice_in_dim(block, core * mine, mine, 1)
    came = lax.ppermute(away, "grid", [(g, g ^ 1) for g in range(columns)])
    field = jnp.where(
        core == 0,
        jnp.concatenate([kept, came], axis=0),
        jnp.concatenate([came, kept], axis=0),
    ).T

    def operator(field):
        scaled = mass * field
        upper = lax.ppermute(scaled[:RIM], BOTH, downs)
        summed = element_sums(jnp.concatenate([scaled, upper], axis=0), index, scale, matrix)
        lower = lax.ppermute(summed[mine:], BOTH, ups)
        assembled = jnp.concatenate([summed[:RIM] + lower, summed[RIM:mine]], axis=0)
        return mass * assembled + pot * field

    first = sigma / half * (operator(field) - centre * field)
    filtered = 2.0 * (sigma_two / half) * (operator(first) - centre * first) - sigma * sigma_two * field
    wide = filtered.T

    blocks = mine // (parts * NB)
    shaped = wide.reshape(2, columns, SB, blocks, parts, NB).transpose(4, 1, 0, 2, 3, 5)
    shaped = shaped.reshape(parts * columns, 2 * SB, blocks * NB)
    moved = lax.all_to_all(shaped, BOTH, split_axis=0, concat_axis=0, tiled=True)
    cyclic = (
        moved.reshape(parts, columns // 2, 2, 2 * SB, blocks * NB)
        .transpose(1, 3, 0, 2, 4)
        .reshape(states, owned)
    )

    y = lax.axis_index("grid") // 2
    quarter = mine // 2
    over = lax.dynamic_slice_in_dim(wide, (1 - y) * quarter, quarter, 1)
    stay = lax.dynamic_slice_in_dim(wide, y * quarter, quarter, 1)
    other = lax.ppermute(over, "grid", [(g, g ^ 2) for g in range(columns)])
    whole = jnp.where(
        y == 0, jnp.concatenate([stay, other], axis=0), jnp.concatenate([other, stay], axis=0)
    )
    gram = jnp.dot(whole, whole.T, precision=lax.Precision.HIGHEST) * (1.0 / (owned * parts))
    gram = lax.psum(gram, BOTH)
    count = columns * states
    gram = gram.reshape(columns, columns, SB, columns, columns, SB)
    gram = gram.transpose(1, 0, 2, 4, 3, 5).reshape(count, count)
    panel = lax.dynamic_slice_in_dim(gram, lax.axis_index("grid") * states, states, 1)
    return cyclic, panel


def solution(mesh):
    placed = (P("grid", "nodes"), P("nodes"), P("nodes"), P("nodes"), P("nodes", None), P())
    return jax.shard_map(
        shards,
        mesh=mesh,
        in_specs=placed,
        out_specs=(P("grid", "nodes"), P(None, "grid")),
        check_vma=False,
    )
```

time: 616 us -> 345 us (0.56)
  other arithmetic: 192 us -> 15 us
  local copies, waits for them, and re-layouts: 137 us -> 28.8 us
  blocking collectives: 78.4 us -> 0 us
  starting transfers between devices: 12 us -> 52.9 us
  Pallas kernels: 0 us -> 40.7 us
  waiting for transfers between devices: 157 us -> 190 us
  matrix products: 23.8 us -> 3.51 us
    scatter-add x2 -> x0, other arithmetic: 181 us -> none  [apply_operator(): summed = jnp.zeros(wide.shape, jnp.float32).at[:, conn_t].add(local)]
    gather x4 -> x0, local copies, waits for them, and re-layouts: 83.4 us -> none  [apply_operator(): picked = wide[:, conn_t]]
    all_to_all x2 -> x0, blocking collectives: 78.4 us -> none  [the longest x1 50.2 us: shards(): lax.all_to_all(shaped, 'nodes', split_axis=2, concat_axis=2, tiled=True)]
    psum x1, waiting for transfers between devices: 68.6 us -> 125 us  [shards(): gram = lax.psum(gram, BOTH)]
    all_gather x1 -> x0, waiting for transfers between devices: 56.5 us -> none  [shards(): lax.all_gather(cyclic, 'grid', axis=0, tiled=True)]
    pallas_call x0 -> x2, Pallas kernels: none -> 40.7 us  [element_sums(): pl.pallas_call(functools.partial(operator_kernel, npe), out_shape=jax.Sha...]
    ppermute x4 -> x6, waiting for transfers between devices: 31.9 us -> 64.7 us  [the longest x1 44.8 us: shards(): other = lax.ppermute(over, 'grid', [(g, g ^ 2) for g in range(columns)])]
    ppermute x4 -> x6, starting transfers between devices: 11.9 us -> 34.5 us  [the longest x2 29.7 us: operator(): lower = lax.ppermute(summed[mine:], BOTH, ups)]
  transfers between devices with their start and end apart: 6 -> 8, of which waited for: 6 -> 7; matrix products, arithmetic and copies ran while one was open for 3% -> 5% of each run, Pallas kernels for 0% -> 0%
where the time goes in v1:
time: 345 us
  waiting for transfers between devices  190 us (55%)
  starting transfers between devices  52.9 us (15%)
  Pallas kernels  40.7 us (12%)
  local copies, waits for them, and re-layouts  28.8 us (8%)
  other arithmetic  15 us (4%)
  between operations  14.4 us (4%)
  matrix products  3.51 us (1%)
    psum x1, waiting for transfers between devices, shards(): gram = lax.psum(gram, BOTH)  125 us
    ppermute x1, waiting for transfers between devices, shards(): other = lax.ppermute(over, 'grid', [(g, g ^ 2) for g in range(columns)])  44.8 us
    pallas_call x2, Pallas kernels, element_sums(): pl.pallas_call(functools.partial(operator_kernel, npe), out_shape=jax.Sha...  40.7 us
    ppermute x2, starting transfers between devices, operator(): lower = lax.ppermute(summed[mine:], BOTH, ups)  29.7 us
    all_to_all x1, starting transfers between devices, shards(): lax.all_to_all(shaped, BOTH, split_axis=0, concat_axis=0, tiled=True)  18.4 us
    ppermute x2, waiting for transfers between devices, operator(): upper = lax.ppermute(scaled[:RIM], BOTH, downs)  15.3 us
    mul x3, other arithmetic, operator(): scaled = mass * field  7.43 us
  transfers between devices with their start and end apart: 8, of which 7 were waited for; matrix products, arithmetic and copies ran while one was open for 5% of the time, Pallas kernels for 0%

profile of v1, /device:TPU:0, one launch (start us, length us, event | category | flops | bytes accessed | tf_op | source)
XLA Modules:
  0.0 345.1 jit_solution(12839301432394964399)
XLA Ops:
  7.2 1.7 constant_dynamic-slice_fusion.1
  8.9 0.0 copy-start.4
  8.9 0.5 collective-permute-start
  9.4 1.9 copy.29
  11.3 0.0 copy-done.4
  11.4 0.4 collective-permute-done
  11.7 1.9 copy.23
  13.6 5.5 %multiply_bitcast_fusion = (f32[4096,128]{1,0:T(8,128)S(1)}, f32[128,4096]{0,1:T(8,128)S(1)}) fusion(f32[4096]{0:T(1024)S(1)} %get-tuple-element.5, f32[64,4096]{0,1:T(8,128)} %copy.29, f32[64,4096]{0,1:T(8,128)} %copy.23, pred[]{:T(512)S(6)} %eq.8), kind=kLoop, calls=%fused_computation.18 | loop fusion | flops 2097152 | bytes 6307841 | tf_op jit(solution)/shard_map/mul | solution.py:118
  19.1 0.0 copy-start.1
  19.1 0.0 copy-start.6
  19.2 0.0 copy-start.3
  19.2 0.0 copy-start.2
  19.2 1.3 copy-done.1
  20.5 0.1 slice.32
  20.5 1.3 collective-permute-start.1
  21.8 0.0 copy-done.6
  21.8 0.1 dynamic_slice.29.scale_ref
  21.9 0.0 copy-done.3
  21.9 0.1 reshape.28.index_ref
  22.1 0.0 copy-done.2
  22.1 3.1 collective-permute-done.1
  25.2 2.1 pad_maximum_fusion.wide_ref
  27.3 20.4 %shard_map.77 = f32[6144,128]{1,0:T(8,128)S(1)} custom-call(s32[8000]{0:T(1024)S(1)} %reshape.28.index_ref, f32[64]{0:T(128)S(1)} %dynamic_slice.29.scale_ref, f32[128,128]{1,0:T(8,128)S(1)} %pad.4.matrix_ref, f32[6144,128]{1,0:T(8,128)S(1)} %pad_maximum_fusion.wide_ref), custom_call_target="tpu_custom_call" | custom-call | tf_op jit(solution)/shard_map/pallas_call | solution.py:69
  47.7 0.0 copy-start.5
  47.7 0.1 slice.34
  47.8 14.8 %collective-permute-start.2 = (f32[2048,128]{1,0:T(8,128)S(1)}, f32[2048,128]{1,0:T(8,128)S(1)}, u32[]{:S(2)}, u32[]{:S(2)}) collective-permute-start(f32[2048,128]{1,0:T(8,128)S(1)} %slice.34), channel_id=1, source_target_pairs={{0,1},{1,4},{4,5},{5,8},{8,9},{9,12},{12,13},{13,16},{16,17},{17,2... | collective-permute-start | bytes 3145736 | tf_op jit(solution)/shard_map/ppermute | solution.py:121
  62.6 0.0 copy-done.5
  62.6 2.2 collective-permute-done.2
  64.8 0.2 slice_add_fusion.1
  64.9 1.9 fusion.13
  66.9 0.1 slice.36
  67.0 1.3 collective-permute-start.3
  68.3 12.2 %collective-permute-done.3 = f32[2048,128]{1,0:T(8,128)S(1)} collective-permute-done((f32[2048,128]{1,0:T(8,128)S(1)}, f32[2048,128]{1,0:T(8,128)S(1)}, u32[]{:S(2)}, u32[]{:S(2)}) %collective-permute-start.3) | collective-permute-done | bytes 1048608 | tf_op jit(solution)/shard_map/ppermute | solution.py:119
  80.5 0.2 pad_maximum_fusion.1.wide_ref
  80.7 20.4 %shard_map.78 = f32[6144,128]{1,0:T(8,128)S(1)} custom-call(s32[8000]{0:T(1024)S(1)} %reshape.28.index_ref, f32[64]{0:T(128)S(1)} %dynamic_slice.29.scale_ref, f32[128,128]{1,0:T(8,128)S(1)} %pad.4.matrix_ref, f32[6144,128]{1,0:T(8,128)S(1)} %pad_maximum_fusion.1.wide_ref), custom_call_target="tpu_custom_call" | custom-call | tf_op jit(solution)/shard_map/pallas_call | solution.py:69
  101.1 0.1 slice.38
  101.2 14.9 %collective-permute-start.4 = (f32[2048,128]{1,0:T(8,128)S(1)}, f32[2048,128]{1,0:T(8,128)S(1)}, u32[]{:S(2)}, u32[]{:S(2)}) collective-permute-start(f32[2048,128]{1,0:T(8,128)S(1)} %slice.38), channel_id=1, source_target_pairs={{0,1},{1,4},{4,5},{5,8},{8,9},{9,12},{12,13},{13,16},{16,17},{17,2... | collective-permute-start | bytes 3145736 | tf_op jit(solution)/shard_map/ppermute | solution.py:121
  116.1 2.0 collective-permute-done.4
  118.1 0.2 slice_add_fusion
  118.3 4.8 %fusion.5 = f32[4096,128]{1,0:T(8,128)} fusion(f32[2048,128]{1,0:T(8,128)S(1)} %get-tuple-element.9, f32[2048,128]{1,0:T(8,128)S(1)} %get-tuple-element.8, f32[128,4096]{0,1:T(8,128)S(1)} %get-tuple-element.7, f32[2048,128]{1,0:T(8,128)S(1)} %get-tuple-element.11, f32[2048,128]{1,0:T(8,128)S(1)} %get-tuple-element.10, f32[4096]{0:T(1024)S(1)} %get-tuple-element.2, ...), kind=kLoop, calls=%fused_computation.10 | loop fusion | flops 7864320 | bytes 8437760 | tf_op jit(solution)/shard_map/sub | solution.py:126
  123.1 1.9 copy.25
  125.1 0.4 copy.30
  125.4 0.5 copy.26
  126.0 1.8 reshape.30
  127.9 0.0 copy-start
  127.9 18.4 %all-to-all-start = ((f32[32,32,512]{2,1,0:T(8,128)}), f32[32,32,512]{2,1,0:T(8,128)}, u32[]{:S(2)}, u32[]{:S(2)}) async-start(f32[32,32,512]{2,1,0:T(8,128)} %reshape.30), calls=%async_computation | async-start | bytes 4194304 | tf_op jit(solution)/shard_map/all_to_all | solution.py:132
  146.3 0.0 all-reduce.3.cloned.1.call-start
  146.3 0.0 copy-done
  146.4 1.1 dynamic-slice_bitcast_fusion.1
  147.5 1.7 collective-permute-start.5
  149.2 44.8 %collective-permute-done.5 = f32[128,2048]{0,1:T(8,128)S(1)} collective-permute-done((f32[128,2048]{0,1:T(8,128)}, f32[128,2048]{0,1:T(8,128)S(1)}, u32[]{:S(2)}, u32[]{:S(2)}) %collective-permute-start.5) | collective-permute-done | bytes 1048608 | tf_op jit(solution)/shard_map/ppermute | solution.py:143
  193.9 3.5 %fusion.12 = f32[256,256]{1,0:T(8,128)S(1)} fusion(f32[128,2048]{0,1:T(8,128)S(1)} %collective-permute-done.5, f32[128,2048]{0,1:T(8,128)S(1)} %get-tuple-element.12, pred[]{:T(512)S(6)} %eq.9), kind=kOutput, calls=%fused_computation.19 | convolution fusion | flops 1612251136 | bytes 2359297 | tf_op jit(solution)/shard_map/dot_general | solution.py:147
  197.5 1.5 reshape.33
  198.9 2.6 copy.28
  201.6 4.0 %reshape.34 = f32[256,256]{0,1:T(8,128)} reshape(f32[4,4,16,4,4,16]{2,1,0,5,4,3:T(4,128)} %copy.28) | data formatting | bytes 524288 | tf_op jit(solution)/shard_map/reshape | solution.py:151
  205.6 0.0 all-reduce.3.cloned.1.call-update
  205.6 125.1 %all-reduce.3.cloned.1.call-done = f32[256,256]{0,1:T(8,128)} async-done(((f32[256,256]{0,1:T(8,128)}), f32[256,256]{0,1:T(8,128)}) %all-reduce.3.cloned.1.call-update) | async-done | bytes 262160 | tf_op jit(solution)/shard_map/psum | solution.py:148
  330.7 1.5 constant_dynamic-slice_fusion
  332.2 0.0 all-to-all-done
  332.2 3.2 copy.27
  335.4 2.8 reshape.32
  (4 shorter events, 0.0 us)
Async XLA Ops:
  8.9 2.5 copy-start.4
  8.9 2.8 collective-permute-start
  19.1 1.3 copy-start.1
  19.1 2.7 copy-start.6
  19.2 2.8 copy-start.3
  19.2 2.9 copy-start.2
  20.5 4.7 %collective-permute-start.1 = (f32[2048,128]{1,0:T(8,128)S(1)}, f32[2048,128]{1,0:T(8,128)}, u32[]{:S(2)}, u32[]{:S(2)}) collective-permute-start(f32[2048,128]{1,0:T(8,128)S(1)} %slice.32), channel_id=1, source_target_pairs={{1,0},{4,1},{5,4},{8,5},{9,8},{12,9},{13,12},{16,13},{17,16},{20,1... | collective-permute-start | bytes 3145736 | tf_op jit(solution)/shard_map/ppermute | solution.py:119
  47.7 14.9 %copy-start.5 = (f32[8192]{0:T(1024)S(1)}, f32[8192]{0:T(1024)}, u32[]{:S(2)}) copy-start(f32[8192]{0:T(1024)} %param.8) | copy-start | bytes 98308
  47.8 17.0 %collective-permute-start.2 = (f32[2048,128]{1,0:T(8,128)S(1)}, f32[2048,128]{1,0:T(8,128)S(1)}, u32[]{:S(2)}, u32[]{:S(2)}) collective-permute-start(f32[2048,128]{1,0:T(8,128)S(1)} %slice.34), channel_id=1, source_target_pairs={{0,1},{1,4},{4,5},{5,8},{8,9},{9,12},{12,13},{13,16},{16,17},{17,2... | collective-permute-start | bytes 3145736 | tf_op jit(solution)/shard_map/ppermute | solution.py:121
  67.0 13.5 %collective-permute-start.3 = (f32[2048,128]{1,0:T(8,128)S(1)}, f32[2048,128]{1,0:T(8,128)S(1)}, u32[]{:S(2)}, u32[]{:S(2)}) collective-permute-start(f32[2048,128]{1,0:T(8,128)S(1)} %slice.36), channel_id=1, source_target_pairs={{1,0},{4,1},{5,4},{8,5},{9,8},{12,9},{13,12},{16,13},{17,16},{20,1... | collective-permute-start | bytes 3145736 | tf_op jit(solution)/shard_map/ppermute | solution.py:119
  101.2 17.0 %collective-permute-start.4 = (f32[2048,128]{1,0:T(8,128)S(1)}, f32[2048,128]{1,0:T(8,128)S(1)}, u32[]{:S(2)}, u32[]{:S(2)}) collective-permute-start(f32[2048,128]{1,0:T(8,128)S(1)} %slice.38), channel_id=1, source_target_pairs={{0,1},{1,4},{4,5},{5,8},{8,9},{9,12},{12,13},{13,16},{16,17},{17,2... | collective-permute-start | bytes 3145736 | tf_op jit(solution)/shard_map/ppermute | solution.py:121
  127.9 18.5 %copy-start = (f32[4096,128]{1,0:T(8,128)S(1)}, f32[4096,128]{1,0:T(8,128)}, u32[]{:S(2)}) copy-start(f32[4096,128]{1,0:T(8,128)} %fusion.5) | copy-start | bytes 6291460
  127.9 204.4 %all-to-all-start = ((f32[32,32,512]{2,1,0:T(8,128)}), f32[32,32,512]{2,1,0:T(8,128)}, u32[]{:S(2)}, u32[]{:S(2)}) async-start(f32[32,32,512]{2,1,0:T(8,128)} %reshape.30), calls=%async_computation | async-start | bytes 4194304 | tf_op jit(solution)/shard_map/all_to_all | solution.py:132
  146.3 184.5 %all-reduce.3.cloned.1.call-start = ((), (), s32[]{:S(2)}) async-start(), calls=%async_computation.1 | async-start | bytes 524288 | tf_op jit(solution)/shard_map/psum | solution.py:148
  147.5 46.5 %collective-permute-start.5 = (f32[128,2048]{0,1:T(8,128)}, f32[128,2048]{0,1:T(8,128)S(1)}, u32[]{:S(2)}, u32[]{:S(2)}) collective-permute-start(f32[128,2048]{0,1:T(8,128)} %get-tuple-element.13), channel_id=1, source_target_pairs={{0,2},{1,3},{2,0},{3,1},{4,6},{5,7},{6,4},{7,5},{8,10},{9,11},{10,... | collective-permute-start | bytes 3145736 | tf_op jit(solution)/shard_map/ppermute | solution.py:143
Sparse Core Ops, SparseCore 0:
  205.7 124.9 all-reduce.2

commit v2 on v1

--- a/solution.py
+++ b/solution.py
@@ -77,12 +77,268 @@
     )(index.reshape(-1), scale, matrix, wide)
 
 
+STRIDE = 11
+MESH = pl.DeviceIdType.MESH
+
+
+def others(count, me, body):
+    stride = STRIDE if count % STRIDE else 1
+
+    def step(s, carry):
+        body(lax.rem(me + s * stride, count))
+        return carry
+
+    lax.fori_loop(1, count, step, 0)
+
+
+def greet(devices):
+    barrier = pltpu.get_barrier_semaphore()
+    for device in devices:
+        pl.semaphore_signal(barrier, inc=1, device_id=device, device_id_type=MESH)
+    pl.semaphore_wait(barrier, len(devices))
+
+
+def finish_kernel(
+    parts, columns, pieces, weight,
+    sums_ref, one_ref, two_ref, coef_ref, out_ref, panel_ref,
+    flat, send, rim, raw, high, low, gram, collected, stage, panel,
+    rim_sem, swap_sem, move_send, move_recv, part_send, part_recv, row_send, row_recv, own_sem,
+):
+    p, g = lax.axis_index("nodes"), lax.axis_index("grid")
+    y, k = g // 2, lax.rem(g, 2)
+    count = parts * columns
+    me = p * columns + g
+    t, last = 2 * p + k, 2 * parts - 1
+    mine = flat.shape[1]
+    quarter = mine // 4
+    width = mine // parts
+    span = width // pieces
+    states = panel_ref.shape[1]
+    total_states = gram.shape[0]
+    owners = total_states // 8
+
+    def place(d):
+        return (d // columns, lax.rem(d, columns))
+
+    barrier = pltpu.get_barrier_semaphore()
+    others(
+        count, me,
+        lambda d: pl.semaphore_signal(barrier, inc=1, device_id=place(d), device_id_type=MESH),
+    )
+    pl.semaphore_wait(barrier, count - 1)
+
+    def rim_copy():
+        up = t + 1
+        return pltpu.make_async_remote_copy(
+            src_ref=sums_ref.at[pl.ds(mine, RIM)], dst_ref=rim,
+            send_sem=rim_sem.at[0], recv_sem=rim_sem.at[1],
+            device_id=(up // 2, 2 * y + lax.rem(up, 2)), device_id_type=MESH,
+        )
+
+    @pl.when(t < last)
+    def _():
+        rim_copy().start()
+
+    @pl.when(t == 0)
+    def _():
+        rim[...] = jnp.zeros_like(rim)
+
+    def swap_copy(h):
+        start = pl.multiple_of((2 * h + 1 - y) * quarter, 128)
+        return pltpu.make_async_remote_copy(
+            src_ref=flat.at[:, pl.ds(start, quarter)],
+            dst_ref=raw.at[h, pl.ds(pl.multiple_of(y * 128, 128), 128)],
+            send_sem=swap_sem.at[0, h], recv_sem=swap_sem.at[1, h],
+            device_id=(p, 2 * (1 - y) + k), device_id_type=MESH,
+        )
+
+    def landing(d, h):
+        dp, dg = place(d)
+        row = pl.multiple_of((dg // 2) * 32, 32)
+        column = pl.multiple_of((dp * 2 + lax.rem(dg, 2)) * width + h * span, 128)
+        return out_ref.at[pl.ds(row, 32), pl.ds(column, span)]
+
+    def move(d, h, source):
+        return pltpu.make_async_remote_copy(
+            src_ref=send.at[d, :, pl.ds(h * span, span)], dst_ref=landing(source, h),
+            send_sem=move_send.at[h, d], recv_sem=move_recv.at[h, source],
+            device_id=place(d), device_id_type=MESH,
+        )
+
+    def combine(b, with_rim):
+        at = pl.multiple_of(b * 128, 128)
+        rows = pl.ds(at, 128)
+        value = sums_ref[rows, :]
+        if with_rim:
+            value = value + rim[rows, :]
+        result = (
+            value.T * coef_ref[2:3, rows]
+            + two_ref[rows, :].T * coef_ref[3:4, rows]
+            + one_ref[rows, :].T * coef_ref[4:5, rows]
+        )
+        flat[:, rows] = result
+        l, q = b // parts, lax.rem(b, parts)
+        for c in range(columns):
+            for kk in range(2):
+                send[q * columns + c, kk * SB : (kk + 1) * SB, pl.ds(pl.multiple_of(l * 128, 128), 128)] = (
+                    result[kk * states + c * SB : kk * states + (c + 1) * SB, :]
+                )
+
+    half = mine // 256
+
+    def keep(h):
+        start = pl.multiple_of((2 * h + y) * quarter, 128)
+        raw[h, pl.ds(pl.multiple_of(y * 128, 128), 128), :] = flat[:, pl.ds(start, quarter)]
+
+    @pl.loop(half, 2 * half)
+    def _(b):
+        combine(b, False)
+
+    swap_copy(1).start()
+    if pieces == 2:
+        others(count, me, lambda d: move(d, 1, me).start())
+    keep(1)
+
+    @pl.when(t > 0)
+    def _():
+        rim_copy().wait_recv()
+
+    @pl.loop(0, half)
+    def _(b):
+        combine(b, True)
+
+    swap_copy(0).start()
+    others(count, me, lambda d: move(d, 0, me).start())
+    keep(0)
+    own = [
+        pltpu.make_async_copy(send.at[me, :, pl.ds(h * span, span)], landing(me, h), own_sem.at[h])
+        for h in range(pieces)
+    ]
+    for copy in own:
+        copy.start()
+
+    across = (((1,), (1,)), ((), ()))
+
+    def product(a, b):
+        return lax.dot_general(a, b, across, preferred_element_type=jnp.float32)
+
+    for h in (1, 0):
+        swap_copy(h).wait_recv()
+        for c in range(columns):
+            for kb in range(columns):
+                upper, lower = split(raw[h, kb * states + c * SB : kb * states + (c + 1) * SB, :])
+                to = c * states + kb * SB
+                high[to : to + SB, :] = upper
+                low[to : to + SB, :] = lower
+        mixed = product(high[...], low[...])
+        value = product(high[...], high[...]) + (mixed + mixed.T)
+        if h == 1:
+            gram[...] = value
+        else:
+            gram[...] = gram[...] + value
+
+    def rows_of(d):
+        return pl.ds(pl.multiple_of(d * 8, 8), 8)
+
+    def part(d, source):
+        return pltpu.make_async_remote_copy(
+            src_ref=gram.at[rows_of(d)], dst_ref=collected.at[source],
+            send_sem=part_send.at[d], recv_sem=part_recv.at[source],
+            device_id=place(d), device_id_type=MESH,
+        )
+
+    def if_owner(d, body):
+        if owners == count:
+            body()
+        else:
+            pl.when(d < owners)(body)
+
+    def row(d, source):
+        return pltpu.make_async_remote_copy(
+            src_ref=stage.at[lax.rem(d, columns)], dst_ref=panel.at[rows_of(source)],
+            send_sem=row_send.at[d], recv_sem=row_recv.at[source],
+            device_id=place(d), device_id_type=MESH,
+        )
+
+    others(count, me, lambda d: if_owner(d, lambda: part(d, me).start()))
+    stage[...] = jnp.zeros_like(stage)
+
+    def own_rows():
+        collected[me] = gram[rows_of(me), :]
+        others(count, me, lambda d: part(me, d).wait_recv())
+        sums = lax.fori_loop(
+            0, count, lambda d, value: value + collected[d], jnp.zeros(collected.shape[1:], jnp.float32)
+        )
+        sums = sums * weight
+        for c in range(columns):
+            stage[c, :, :states] = sums[:, c * states : (c + 1) * states]
+        panel[rows_of(me), :] = stage[g]
+        others(count, me, lambda d: row(d, me).start())
+
+    if_owner(me, own_rows)
+    others(count, me, lambda d: if_owner(d, lambda: row(me, d).wait_recv()))
+    panel_ref[...] = panel[:, :states]
+
+    for h in range(pieces):
+        others(count, me, lambda d: move(me, h, d).wait_recv())
+    for h in range(pieces):
+        others(count, me, lambda d: move(d, h, me).wait_send())
+    for copy in own:
+        copy.wait()
+    for h in (0, 1):
+        swap_copy(h).wait_send()
+    others(count, me, lambda d: if_owner(d, lambda: part(d, me).wait_send()))
+    if_owner(me, lambda: others(count, me, lambda d: row(d, me).wait_send()))
+
+    @pl.when(t < last)
+    def _():
+        rim_copy().wait_send()
+
+
+def finish(parts, columns, states, owned, sums, one, two, coef):
+    mine = owned // 2
+    count = parts * columns
+    width = mine // parts
+    pieces = 2 if width % 256 == 0 else 1
+    total = columns * states
+    vmem = pl.BlockSpec(memory_space=pltpu.VMEM)
+    dma = pltpu.SemaphoreType.DMA
+    f32, bf16 = jnp.float32, jnp.bfloat16
+    return pl.pallas_call(
+        functools.partial(finish_kernel, parts, columns, pieces, 1.0 / (owned * parts)),
+        out_shape=(
+            jax.ShapeDtypeStruct((states, owned), f32),
+            jax.ShapeDtypeStruct((total, states), f32),
+        ),
+        in_specs=[vmem] * 4,
+        out_specs=(pl.BlockSpec(memory_space=pl.ANY), vmem),
+        scratch_shapes=[
+            pltpu.VMEM((2 * states, mine), f32),
+            pltpu.VMEM((count, 2 * SB, width), f32),
+            pltpu.VMEM((RIM, 2 * states), f32),
+            pltpu.VMEM((2, total, mine // 4), f32),
+            pltpu.VMEM((total, mine // 4), bf16),
+            pltpu.VMEM((total, mine // 4), bf16),
+            pltpu.VMEM((total, total), f32),
+            pltpu.VMEM((count, 8, total), f32),
+            pltpu.VMEM((columns, 8, 128), f32),
+            pltpu.VMEM((total, 128), f32),
+            dma((2,)), dma((2, 2)), dma((pieces, count)), dma((pieces, count)),
+            dma((count,)), dma((count,)), dma((count,)), dma((count,)), dma((pieces,)),
+        ],
+        compiler_params=pltpu.CompilerParams(
+            collective_id=0, has_side_effects=True, vmem_limit_bytes=44 * 1024 * 1024
+        ),
+    )(sums, one, two, coef)
+
+
 def shards(block, inv_sqrt_mass, potential, elem_scale, connectivity, elem_matrix):
     lowest, cut, top = (-2.0, 4.0, 32.0)
     half = (top - cut) / 2.0
     centre = (top + cut) / 2.0
     sigma = half / (lowest - centre)
     sigma_two = 1.0 / (2.0 / sigma - sigma)
+    alpha, beta, gamma = sigma / half, 2.0 * (sigma_two / half), sigma * sigma_two
     parts = lax.axis_size("nodes")
     columns = lax.axis_size("grid")
     states, owned = block.shape
@@ -100,57 +356,45 @@
 
     index = lax.dynamic_slice_in_dim(connectivity, core * elements, elements, 0) - core * mine
     scale = lax.dynamic_slice_in_dim(elem_scale, core * elements, elements, 0)
-    mass = lax.dynamic_slice_in_dim(inv_sqrt_mass, core * mine, mine, 0)[:, None]
-    pot = lax.dynamic_slice_in_dim(potential, core * mine, mine, 0)[:, None]
     pad = -elem_matrix.shape[0] % 128
     matrix = jnp.pad(elem_matrix, ((0, pad), (0, pad)))
 
-    away = lax.dynamic_slice_in_dim(block, (1 - core) * mine, mine, 1)
-    kept = lax.dynamic_slice_in_dim(block, core * mine, mine, 1)
+    shift = potential - centre
+    inverse = 1.0 / inv_sqrt_mass
+    zero = jnp.zeros_like(shift)
+    coef = jnp.stack(
+        [
+            alpha * inv_sqrt_mass * inv_sqrt_mass,
+            alpha * shift,
+            beta * inv_sqrt_mass,
+            beta * shift * inverse,
+            -gamma * inverse,
+            zero,
+            zero,
+            zero,
+        ]
+    )
+    coef = lax.dynamic_slice_in_dim(coef, core * mine, mine, 1)
+    coef = jnp.concatenate([coef, lax.ppermute(coef[:, :RIM], BOTH, downs)], axis=1)
+
+    scaled = inv_sqrt_mass[None, :] * block
+    away = lax.dynamic_slice_in_dim(scaled, (1 - core) * mine, mine, 1)
+    kept = lax.dynamic_slice_in_dim(scaled, core * mine, mine, 1)
     came = lax.ppermute(away, "grid", [(g, g ^ 1) for g in range(columns)])
     field = jnp.where(
         core == 0,
         jnp.concatenate([kept, came], axis=0),
         jnp.concatenate([came, kept], axis=0),
     ).T
-
-    def operator(field):
-        scaled = mass * field
-        upper = lax.ppermute(scaled[:RIM], BOTH, downs)
-        summed = element_sums(jnp.concatenate([scaled, upper], axis=0), index, scale, matrix)
-        lower = lax.ppermute(summed[mine:], BOTH, ups)
-        assembled = jnp.concatenate([summed[:RIM] + lower, summed[RIM:mine]], axis=0)
-        return mass * assembled + pot * field
-
-    first = sigma / half * (operator(field) - centre * field)
-    filtered = 2.0 * (sigma_two / half) * (operator(first) - centre * first) - sigma * sigma_two * field
-    wide = filtered.T
-
-    blocks = mine // (parts * NB)
-    shaped = wide.reshape(2, columns, SB, blocks, parts, NB).transpose(4, 1, 0, 2, 3, 5)
-    shaped = shaped.reshape(parts * columns, 2 * SB, blocks * NB)
-    moved = lax.all_to_all(shaped, BOTH, split_axis=0, concat_axis=0, tiled=True)
-    cyclic = (
-        moved.reshape(parts, columns // 2, 2, 2 * SB, blocks * NB)
-        .transpose(1, 3, 0, 2, 4)
-        .reshape(states, owned)
-    )
-
-    y = lax.axis_index("grid") // 2
-    quarter = mine // 2
-    over = lax.dynamic_slice_in_dim(wide, (1 - y) * quarter, quarter, 1)
-    stay = lax.dynamic_slice_in_dim(wide, y * quarter, quarter, 1)
-    other = lax.ppermute(over, "grid", [(g, g ^ 2) for g in range(columns)])
-    whole = jnp.where(
-        y == 0, jnp.concatenate([stay, other], axis=0), jnp.concatenate([other, stay], axis=0)
-    )
-    gram = jnp.dot(whole, whole.T, precision=lax.Precision.HIGHEST) * (1.0 / (owned * parts))
-    gram = lax.psum(gram, BOTH)
-    count = columns * states
-    gram = gram.reshape(columns, columns, SB, columns, columns, SB)
-    gram = gram.transpose(1, 0, 2, 4, 3, 5).reshape(count, count)
-    panel = lax.dynamic_slice_in_dim(gram, lax.axis_index("grid") * states, states, 1)
-    return cyclic, panel
+    one = jnp.concatenate([field, lax.ppermute(field[:RIM], BOTH, downs)], axis=0)
+
+    sums = element_sums(one, index, scale, matrix)
+    lower = lax.ppermute(sums[mine:], BOTH, ups)
+    upper = lax.ppermute(sums[:RIM], BOTH, downs)
+    assembled = jnp.concatenate([sums[:RIM] + lower, sums[RIM:mine], sums[mine:] + upper], axis=0)
+    two = coef[0][:, None] * assembled + coef[1][:, None] * one
+    sums = element_sums(two, index, scale, matrix)
+    return finish(parts, columns, states, owned, sums, one, two, coef)
 
 
 def solution(mesh):

time: 345 us -> 199 us (0.58)
  waiting for transfers between devices: 190 us -> 5.29 us
  Pallas kernels: 40.7 us -> 146 us
  starting transfers between devices: 52.9 us -> 16.6 us
  local copies, waits for them, and re-layouts: 28.8 us -> 14.6 us
  between operations: 14.4 us -> 0.87 us
  matrix products: 3.51 us -> 0 us
    psum x1 -> x0, waiting for transfers between devices: 125 us -> none  [shards(): gram = lax.psum(gram, BOTH)]
    pallas_call x0 -> x1, Pallas kernels: none -> 105 us  [finish(): pl.pallas_call(functools.partial(finish_kernel, parts, columns, pieces, 1...]
    ppermute x5 -> x4, waiting for transfers between devices: 64.3 us -> 3 us  [the longest x1 2.35 us: shards(): upper = lax.ppermute(sums[:RIM], BOTH, downs)]
    all_to_all x1 -> x0, starting transfers between devices: 18.4 us -> none  [shards(): lax.all_to_all(shaped, BOTH, split_axis=0, concat_axis=0, tiled=True)]
    ppermute x5 -> x4, starting transfers between devices: 34 us -> 16.1 us  [the longest x1 12.1 us: shards(): lower = lax.ppermute(sums[mine:], BOTH, ups)]
    reshape x4 -> x0, local copies, waits for them, and re-layouts: 10.1 us -> none  [the longest x1 4.03 us: shards(): gram = gram.transpose(1, 0, 2, 4, 3, 5).reshape(count, count)]
    transpose x4 -> x0, local copies, waits for them, and re-layouts: 8.31 us -> none  [the longest x1 3.21 us: shards(): cyclic = moved.reshape(parts, columns // 2, 2, 2 * SB, blocks * NB).trans...]
    sub x1 -> x0, other arithmetic: 4.84 us -> none  [shards(): 2.0 * (sigma_two / half) * (operator(first) - centre * first)]
  transfers between devices with their start and end apart: 8 -> 5, of which waited for: 7 -> 3; matrix products, arithmetic and copies ran while one was open for 5% -> 3% of each run, Pallas kernels for 0% -> 10%
where the time goes in v2:
time: 199 us
  Pallas kernels  146 us (73%)
  starting transfers between devices  16.6 us (8%)
  other arithmetic  15.7 us (8%)
  local copies, waits for them, and re-layouts  14.6 us (7%)
  waiting for transfers between devices  5.29 us (3%)
    pallas_call x1, Pallas kernels, finish(): pl.pallas_call(functools.partial(finish_kernel, parts, columns, pieces, 1...  105 us
    pallas_call x2, Pallas kernels, element_sums(): pl.pallas_call(functools.partial(operator_kernel, npe), out_shape=jax.Sha...  40.7 us
    ppermute x1, starting transfers between devices, shards(): lower = lax.ppermute(sums[mine:], BOTH, ups)  12.1 us
    unnamed x10, local copies, waits for them, and re-layouts  5.13 us
    mul x1, other arithmetic, shards(): scaled = inv_sqrt_mass[None, :] * block  4.96 us
    transpose x1, other arithmetic, shards(): field = jnp.where(core == 0, jnp.concatenate([kept, came], axis=0), jnp.c...  4.73 us
    add x1, other arithmetic, shards(): two = coef[0][:, None] * assembled + coef[1][:, None] * one  4.1 us
  transfers between devices with their start and end apart: 5, of which 3 were waited for; matrix products, arithmetic and copies ran while one was open for 3% of the time, Pallas kernels for 10%

profile of v2, /device:TPU:0, one launch (start us, length us, event | category | flops | bytes accessed | tf_op | source)
XLA Modules:
  0.0 198.7 jit_solution(10755933080054373061)
XLA Ops:
  0.6 0.0 copy-start.1
  0.7 3.8 %copy.10 = f32[64,8192]{0,1:T(8,128)} copy(f32[64,8192]{1,0:T(8,128)} %param.6) | data formatting | bytes 4194304 | tf_op args[0]
  4.4 0.0 copy-done.1
  4.5 5.0 %broadcast_multiply_fusion = f32[64,8192]{0,1:T(8,128)S(1)} fusion(f32[64,8192]{0,1:T(8,128)} %copy.10, f32[8192]{0:T(1024)S(1)} %copy-done.1), kind=kLoop, calls=%fused_computation.5 | loop fusion | flops 524288 | bytes 4227072 | tf_op jit(solution)/shard_map/mul | solution.py:380
  9.4 1.6 constant_dynamic-slice_fusion.2
  11.0 0.6 copy.11
  11.6 0.5 collective-permute-start.1
  12.1 2.3 %collective-permute-done.1 = f32[64,4096]{1,0:T(8,128)S(1)} collective-permute-done((f32[64,4096]{1,0:T(8,128)S(1)}, f32[64,4096]{1,0:T(8,128)S(1)}, u32[]{:S(2)}, u32[]{:S(2)}) %collective-permute-start.1) | collective-permute-done | bytes 1048608 | tf_op jit(solution)/shard_map/ppermute | solution.py:383
  14.4 1.9 copy.12
  16.4 0.0 copy-start.2
  16.4 4.7 %fusion.1 = f32[4096,128]{1,0:T(8,128)S(1)} fusion(f32[64,4096]{0,1:T(8,128)} %copy.12, f32[64,4096]{0,1:T(8,128)} %get-tuple-element.6, pred[]{:T(512)S(6)} %eq.5), kind=kLoop, calls=%fused_computation.4 | loop fusion | flops 1572864 | bytes 4194305 | tf_op jit(solution)/shard_map/transpose | solution.py:388
  21.1 0.0 copy-start.3
  21.1 1.0 slice.32
  22.2 1.3 collective-permute-start.2
  23.4 0.0 copy-done.2
  23.5 0.6 broadcast_multiply_fusion.1
  24.1 0.6 stack_broadcast_in_dim.3
  24.7 1.1 stack.27
  25.9 0.6 constant_dynamic-slice_fusion
  26.5 1.3 collective-permute-start
  27.8 0.8 dynamic-slice_subtract_fusion
  28.6 0.1 reshape.11.index_ref
  28.7 0.0 copy-done.3
  28.7 0.1 dynamic_slice.16.scale_ref
  28.8 0.8 pad.4.matrix_ref
  29.7 0.0 collective-permute-done.2
  29.7 0.2 pad_maximum_fusion.wide_ref.one_ref
  29.9 20.4 %shard_map.77 = f32[6144,128]{1,0:T(8,128)S(1)} custom-call(s32[8000]{0:T(1024)S(1)} %reshape.11.index_ref, f32[64]{0:T(128)S(1)} %dynamic_slice.16.scale_ref, f32[128,128]{1,0:T(8,128)S(1)} %pad.4.matrix_ref, f32[6144,128]{1,0:T(8,128)S(1)} %pad_maximum_fusion.wide_ref.one_ref), custom_call_target="tpu_custom_call" | custom-call | tf_op jit(solution)/shard_map/pallas_call | solution.py:69
  50.3 0.1 fusion.4
  50.4 12.1 %collective-permute-start.3 = (f32[2048,128]{1,0:T(8,128)S(1)}, f32[2048,128]{1,0:T(8,128)S(1)}, u32[]{:S(2)}, u32[]{:S(2)}) collective-permute-start(f32[2048,128]{1,0:T(8,128)S(1)} %get-tuple-element.11), channel_id=1, source_target_pairs={{0,1},{1,4},{4,5},{5,8},{8,9},{9,12},{12,13},{13,16},{16,17},{17,2... | collective-permute-start | bytes 3145736 | tf_op jit(solution)/shard_map/ppermute | solution.py:392
  62.5 1.5 collective-permute-start.4
  64.0 0.0 collective-permute-done
  64.0 0.6 collective-permute-done.3
  64.7 2.4 %collective-permute-done.4 = f32[2048,128]{1,0:T(8,128)S(1)} collective-permute-done((f32[2048,128]{1,0:T(8,128)S(1)}, f32[2048,128]{1,0:T(8,128)S(1)}, u32[]{:S(2)}, u32[]{:S(2)}) %collective-permute-start.4) | collective-permute-done | bytes 1048608 | tf_op jit(solution)/shard_map/ppermute | solution.py:393
  67.0 0.3 slice_add_fusion.1
  67.3 4.1 %fusion.wide_ref.two_ref = f32[6144,128]{1,0:T(8,128)S(1)} fusion(f32[2048,128]{1,0:T(8,128)S(1)} %get-tuple-element.9, f32[2048,128]{1,0:T(8,128)S(1)} %get-tuple-element.10, f32[2048,128]{1,0:T(8,128)S(1)} %get-tuple-element.8, f32[6144]{0:T(1024)S(1)} %bitcast.15, f32[6144]{0:T(1024)S(1)} %bitcast.14, f32[2048,128]{1,0:T(8,128)S(1)} %collective-permute-done.2, ...), kind=kLoop, calls=%fused_computation.2 | loop fusion | flops 4718592 | bytes 9486336 | tf_op jit(solution)/shard_map/add | solution.py:395
  71.4 0.0 copy-start
  71.4 20.4 %shard_map.78.sums_ref = f32[6144,128]{1,0:T(8,128)S(1)} custom-call(s32[8000]{0:T(1024)S(1)} %reshape.11.index_ref, f32[64]{0:T(128)S(1)} %dynamic_slice.16.scale_ref, f32[128,128]{1,0:T(8,128)S(1)} %pad.4.matrix_ref, f32[6144,128]{1,0:T(8,128)S(1)} %fusion.wide_ref.two_ref), custom_call_target="tpu_custom_call" | custom-call | tf_op jit(solution)/shard_map/pallas_call | solution.py:69
  91.8 0.0 copy-done
  91.8 104.8 %shard_map.79 = (f32[64,8192]{1,0:T(8,128)S(1)}, f32[256,64]{1,0:T(8,128)S(1)}) custom-call(f32[6144,128]{1,0:T(8,128)S(1)} %shard_map.78.sums_ref, f32[6144,128]{1,0:T(8,128)S(1)} %pad_maximum_fusion.wide_ref.one_ref, f32[6144,128]{1,0:T(8,128)} %copy-done, f32[8,6144]{1,0:T(8,128)S(1)} %pad_maximum_fusion.1.coef_ref), custom_call_target="tpu_custom_call" | custom-call | tf_op jit(solution)/shard_map/pallas_call | solution.py:307
  196.7 0.7 copy.14
  197.4 1.3 copy.16
  (4 shorter events, 0.1 us)
Async XLA Ops:
  0.6 3.8 %copy-start.1 = (f32[8192]{0:T(1024)S(1)}, f32[8192]{0:T(1024)}, u32[]{:S(2)}) copy-start(f32[8192]{0:T(1024)} %param.7) | copy-start | bytes 98308
  11.6 2.8 %collective-permute-start.1 = (f32[64,4096]{1,0:T(8,128)S(1)}, f32[64,4096]{1,0:T(8,128)S(1)}, u32[]{:S(2)}, u32[]{:S(2)}) collective-permute-start(f32[64,4096]{1,0:T(8,128)S(1)} %copy.11), channel_id=1, source_target_pairs={{0,1},{1,0},{2,3},{3,2},{4,5},{5,4},{6,7},{7,6},{8,9},{9,8},{10,11... | collective-permute-start | bytes 3145736 | tf_op jit(solution)/shard_map/ppermute | solution.py:383
  16.4 7.1 %copy-start.2 = (f32[8192]{0:T(1024)S(1)}, f32[8192]{0:T(1024)}, u32[]{:S(2)}) copy-start(f32[8192]{0:T(1024)} %param.8) | copy-start | bytes 98308
  21.1 7.6 %copy-start.3 = (f32[128]{0:T(128)S(1)}, f32[128]{0:T(128)}, u32[]{:S(2)}) copy-start(f32[128]{0:T(128)} %param.9) | copy-start | bytes 1540
  22.2 7.5 %collective-permute-start.2 = (f32[2048,128]{1,0:T(8,128)}, f32[2048,128]{1,0:T(8,128)S(1)}, u32[]{:S(2)}, u32[]{:S(2)}) collective-permute-start(f32[2048,128]{1,0:T(8,128)} %slice.32), channel_id=1, source_target_pairs={{1,0},{4,1},{5,4},{8,5},{9,8},{12,9},{13,12},{16,13},{17,16},{20,1... | collective-permute-start | bytes 3145736 | tf_op jit(solution)/shard_map/ppermute | solution.py:389
  26.5 37.5 %collective-permute-start = (f32[8,2048]{1,0:T(8,128)}, f32[8,2048]{1,0:T(8,128)S(1)}, u32[]{:S(2)}, u32[]{:S(2)}) collective-permute-start(f32[8,2048]{1,0:T(8,128)} %constant_dynamic-slice_fusion), channel_id=1, source_target_pairs={{1,0},{4,1},{5,4},{8,5},{9,8},{12,9},{13,12},{16,13},{17,16},{20,1... | collective-permute-start | bytes 196616 | tf_op jit(solution)/shard_map/ppermute | solution.py:378
  50.4 14.3 %collective-permute-start.3 = (f32[2048,128]{1,0:T(8,128)S(1)}, f32[2048,128]{1,0:T(8,128)S(1)}, u32[]{:S(2)}, u32[]{:S(2)}) collective-permute-start(f32[2048,128]{1,0:T(8,128)S(1)} %get-tuple-element.11), channel_id=1, source_target_pairs={{0,1},{1,4},{4,5},{5,8},{8,9},{9,12},{12,13},{13,16},{16,17},{17,2... | collective-permute-start | bytes 3145736 | tf_op jit(solution)/shard_map/ppermute | solution.py:392
  62.5 4.6 %collective-permute-start.4 = (f32[2048,128]{1,0:T(8,128)S(1)}, f32[2048,128]{1,0:T(8,128)S(1)}, u32[]{:S(2)}, u32[]{:S(2)}) collective-permute-start(f32[2048,128]{1,0:T(8,128)S(1)} %get-tuple-element.12), channel_id=1, source_target_pairs={{1,0},{4,1},{5,4},{8,5},{9,8},{12,9},{13,12},{16,13},{17,16},{20,1... | collective-permute-start | bytes 3145736 | tf_op jit(solution)/shard_map/ppermute | solution.py:393
  71.4 20.4 %copy-start = (f32[6144,128]{1,0:T(8,128)}, f32[6144,128]{1,0:T(8,128)S(1)}, u32[]{:S(2)}) copy-start(f32[6144,128]{1,0:T(8,128)S(1)} %fusion.wide_ref.two_ref) | copy-start | bytes 9437188

commit v3 on v2

--- a/solution.py
+++ b/solution.py
@@ -10,7 +10,7 @@
 NB = 128
 SB = 16
 GROUP = 4
-CHAINS = 4
+CHAINS = 8
 BOTH = ("nodes", "grid")
 
 
@@ -81,21 +81,14 @@
 MESH = pl.DeviceIdType.MESH
 
 
-def others(count, me, body):
+def others(count, me, body, begin=1, end=None):
     stride = STRIDE if count % STRIDE else 1
 
     def step(s, carry):
         body(lax.rem(me + s * stride, count))
         return carry
 
-    lax.fori_loop(1, count, step, 0)
-
-
-def greet(devices):
-    barrier = pltpu.get_barrier_semaphore()
-    for device in devices:
-        pl.semaphore_signal(barrier, inc=1, device_id=device, device_id_type=MESH)
-    pl.semaphore_wait(barrier, len(devices))
+    lax.fori_loop(begin, end or count, step, 0)
 
 
 def finish_kernel(
@@ -172,9 +165,9 @@
         if with_rim:
             value = value + rim[rows, :]
         result = (
-            value.T * coef_ref[2:3, rows]
-            + two_ref[rows, :].T * coef_ref[3:4, rows]
-            + one_ref[rows, :].T * coef_ref[4:5, rows]
+            value.T * coef_ref[3:4, rows]
+            + two_ref[rows, :].T * coef_ref[4:5, rows]
+            + one_ref[rows, :].T * coef_ref[5:6, rows]
         )
         flat[:, rows] = result
         l, q = b // parts, lax.rem(b, parts)
@@ -208,7 +201,7 @@
         combine(b, True)
 
     swap_copy(0).start()
-    others(count, me, lambda d: move(d, 0, me).start())
+    others(count, me, lambda d: move(d, 0, me).start(), 1, count // 2)
     keep(0)
     own = [
         pltpu.make_async_copy(send.at[me, :, pl.ds(h * span, span)], landing(me, h), own_sem.at[h])
@@ -261,6 +254,7 @@
         )
 
     others(count, me, lambda d: if_owner(d, lambda: part(d, me).start()))
+    others(count, me, lambda d: move(d, 0, me).start(), count // 2, count)
     stage[...] = jnp.zeros_like(stage)
 
     def own_rows():
@@ -332,6 +326,218 @@
     )(sums, one, two, coef)
 
 
+def seat(columns):
+    p, g = lax.axis_index("nodes"), lax.axis_index("grid")
+    return p, g, g // 2, lax.rem(g, 2)
+
+
+def remote(source, target, sems, slot, device):
+    return pltpu.make_async_remote_copy(
+        src_ref=source, dst_ref=target, send_sem=sems.at[0, slot], recv_sem=sems.at[1, slot],
+        device_id=device, device_id_type=MESH,
+    )
+
+
+def spread_kernel(
+    parts, columns, block_ref, coef_ref, one_ref, wide_ref, scaled, whole, tail, sems
+):
+    p, g, y, k = seat(columns)
+    states, owned = block_ref.shape
+    mine = owned // 2
+    barrier = pltpu.get_barrier_semaphore()
+    pl.semaphore_signal(barrier, inc=1, device_id=(p, 2 * y + 1 - k), device_id_type=MESH)
+
+    @pl.when(p > 0)
+    def _():
+        pl.semaphore_signal(barrier, inc=1, device_id=(p - 1, 2 * y + 1), device_id_type=MESH)
+
+    @pl.when((k == 1) & (p < parts - 1))
+    def _():
+        for kk in range(2):
+            pl.semaphore_signal(barrier, inc=1, device_id=(p + 1, 2 * y + kk), device_id_type=MESH)
+
+    rows = pl.ds(pl.multiple_of(k * states, 8), states)
+
+    @pl.loop(0, owned // 512)
+    def _(b):
+        at = pl.ds(pl.multiple_of(b * 512, 128), 512)
+        scaled[:, at] = block_ref[:, at] * coef_ref[0:1, at]
+
+    before = jnp.where(p > 0, 1, 0)
+    after = jnp.where((k == 1) & (p < parts - 1), 2, 0)
+    pl.semaphore_wait(barrier, 1 + before + after)
+
+    def back(r=rows, slot=0):
+        return remote(scaled.at[:, pl.ds(0, RIM)], tail.at[r], sems, slot, (p - 1, 2 * y + 1))
+
+    def back_coef():
+        return remote(
+            coef_ref.at[:, pl.ds(0, RIM)], wide_ref.at[:, pl.ds(mine, RIM)], sems, 2,
+            (p - 1, 2 * y + 1),
+        )
+
+    def to_second():
+        return remote(
+            scaled.at[:, pl.ds(mine, mine)], whole.at[rows, pl.ds(0, mine)], sems, 3,
+            (p, 2 * y + 1),
+        )
+
+    def to_first():
+        return remote(
+            scaled.at[:, pl.ds(0, mine + RIM)], whole.at[rows], sems, 4, (p, 2 * y)
+        )
+
+    first, second = k == 0, k == 1
+    at_first, at_second = pl.ds(0, states), pl.ds(states, states)
+    pl.when((p > 0) & first)(lambda: back(at_first, 0).start())
+    pl.when((p > 0) & second)(lambda: back(at_second, 1).start())
+    pl.when((p > 0) & first)(lambda: back_coef().start())
+    pl.when(first)(lambda: to_second().start())
+    pl.when(second)(lambda: to_first().start())
+
+    @pl.when(first)
+    def _():
+        whole[0:states, :] = scaled[:, : mine + RIM]
+        wide_ref[...] = coef_ref[:, : mine + RIM]
+        to_first().wait_recv()
+
+    @pl.when(second)
+    def _():
+        whole[states:, :mine] = scaled[:, mine:]
+        wide_ref[:, :mine] = coef_ref[:, mine:]
+        to_second().wait_recv()
+
+    @pl.loop(0, mine // 128)
+    def _(b):
+        at = pl.ds(pl.multiple_of(b * 128, 128), 128)
+        one_ref[at, :] = whole[:, at].T
+
+    @pl.when(first)
+    def _():
+        @pl.loop(mine // 128, (mine + RIM) // 128)
+        def _(b):
+            at = pl.ds(pl.multiple_of(b * 128, 128), 128)
+            one_ref[at, :] = whole[:, at].T
+
+    @pl.when(second & (p == parts - 1))
+    def _():
+        tail[...] = jnp.zeros_like(tail)
+        wide_ref[:, mine:] = jnp.zeros((wide_ref.shape[0], RIM), jnp.float32)
+
+    @pl.when(second & (p < parts - 1))
+    def _():
+        back(at_first, 0).wait_recv()
+        back(at_second, 1).wait_recv()
+        back_coef().wait_recv()
+
+    @pl.when(second)
+    def _():
+        @pl.loop(0, RIM // 128)
+        def _(b):
+            at = pl.multiple_of(b * 128, 128)
+            one_ref[pl.ds(mine + at, 128), :] = tail[:, pl.ds(at, 128)].T
+
+    pl.when((p > 0) & first)(lambda: back(at_first, 0).wait_send())
+    pl.when((p > 0) & second)(lambda: back(at_second, 1).wait_send())
+    pl.when((p > 0) & first)(lambda: back_coef().wait_send())
+    pl.when(first)(lambda: to_second().wait_send())
+    pl.when(second)(lambda: to_first().wait_send())
+
+
+def spread(parts, columns, block, coef):
+    states, owned = block.shape
+    mine = owned // 2
+    vmem = pl.BlockSpec(memory_space=pltpu.VMEM)
+    f32 = jnp.float32
+    return pl.pallas_call(
+        functools.partial(spread_kernel, parts, columns),
+        out_shape=(
+            jax.ShapeDtypeStruct((mine + RIM, 2 * states), f32),
+            jax.ShapeDtypeStruct((coef.shape[0], mine + RIM), f32),
+        ),
+        in_specs=[vmem] * 2,
+        out_specs=(vmem, vmem),
+        scratch_shapes=[
+            pltpu.VMEM((states, owned), f32),
+            pltpu.VMEM((2 * states, mine + RIM), f32),
+            pltpu.VMEM((2 * states, RIM), f32),
+            pltpu.SemaphoreType.DMA((2, 5)),
+        ],
+        compiler_params=pltpu.CompilerParams(
+            collective_id=1, has_side_effects=True, vmem_limit_bytes=44 * 1024 * 1024
+        ),
+    )(block, coef)
+
+
+def middle_kernel(parts, columns, sums_ref, one_ref, coef_ref, two_ref, lower, upper, sems):
+    p, g, y, k = seat(columns)
+    t, last = 2 * p + k, 2 * parts - 1
+    mine = sums_ref.shape[0] - RIM
+
+    def device(t):
+        return (t // 2, 2 * y + lax.rem(t, 2))
+
+    barrier = pltpu.get_barrier_semaphore()
+    has_up, has_down = t < last, t > 0
+    for have, to in ((has_up, t + 1), (has_down, t - 1)):
+        pl.when(have)(
+            lambda to=to: pl.semaphore_signal(
+                barrier, inc=1, device_id=device(to), device_id_type=MESH
+            )
+        )
+    pl.semaphore_wait(barrier, jnp.where(has_up, 1, 0) + jnp.where(has_down, 1, 0))
+
+    def rise():
+        return remote(sums_ref.at[pl.ds(mine, RIM)], lower, sems, 0, device(t + 1))
+
+    def fall():
+        return remote(sums_ref.at[pl.ds(0, RIM)], upper, sems, 1, device(t - 1))
+
+    pl.when(has_up)(lambda: rise().start())
+    pl.when(has_down)(lambda: fall().start())
+
+    @pl.when(t == 0)
+    def _():
+        lower[...] = jnp.zeros_like(lower)
+
+    @pl.when(t == last)
+    def _():
+        upper[...] = jnp.zeros_like(upper)
+
+    def combine(b, extra, base):
+        rows = pl.ds(pl.multiple_of(b * 128, 128), 128)
+        value = sums_ref[rows, :]
+        if extra is not None:
+            value = value + extra[pl.ds(pl.multiple_of((b - base) * 128, 128), 128), :]
+        size = (128, 128)
+        one = jnp.broadcast_to(coef_ref[1:2, rows], size).T
+        two = jnp.broadcast_to(coef_ref[2:3, rows], size).T
+        two_ref[rows, :] = one * value + two * one_ref[rows, :]
+
+    pl.loop(RIM // 128, mine // 128)(lambda b: combine(b, None, 0))
+    pl.when(has_down)(lambda: rise().wait_recv())
+    pl.loop(0, RIM // 128)(lambda b: combine(b, lower, 0))
+    pl.when(has_up)(lambda: fall().wait_recv())
+    pl.loop(mine // 128, (mine + RIM) // 128)(lambda b: combine(b, upper, mine // 128))
+    pl.when(has_up)(lambda: rise().wait_send())
+    pl.when(has_down)(lambda: fall().wait_send())
+
+
+def middle(parts, columns, sums, one, coef):
+    vmem = pl.BlockSpec(memory_space=pltpu.VMEM)
+    rim = pltpu.VMEM((RIM, sums.shape[1]), jnp.float32)
+    return pl.pallas_call(
+        functools.partial(middle_kernel, parts, columns),
+        out_shape=jax.ShapeDtypeStruct(sums.shape, jnp.float32),
+        in_specs=[vmem] * 3,
+        out_specs=vmem,
+        scratch_shapes=[rim, rim, pltpu.SemaphoreType.DMA((2, 2))],
+        compiler_params=pltpu.CompilerParams(
+            collective_id=2, has_side_effects=True, vmem_limit_bytes=44 * 1024 * 1024
+        ),
+    )(sums, one, coef)
+
+
 def shards(block, inv_sqrt_mass, potential, elem_scale, connectivity, elem_matrix):
     lowest, cut, top = (-2.0, 4.0, 32.0)
     half = (top - cut) / 2.0
@@ -345,15 +551,6 @@
     mine = owned // 2
     core = lax.axis_index("grid") % 2
     elements = connectivity.shape[0] // 2
-
-    ups, downs = [], []
-    for y in range(columns // 2):
-        for t in range(2 * parts - 1):
-            a = (t // 2) * columns + 2 * y + t % 2
-            b = ((t + 1) // 2) * columns + 2 * y + (t + 1) % 2
-            ups.append((a, b))
-            downs.append((b, a))
-
     index = lax.dynamic_slice_in_dim(connectivity, core * elements, elements, 0) - core * mine
     scale = lax.dynamic_slice_in_dim(elem_scale, core * elements, elements, 0)
     pad = -elem_matrix.shape[0] % 128
@@ -364,6 +561,7 @@
     zero = jnp.zeros_like(shift)
     coef = jnp.stack(
         [
+            inv_sqrt_mass,
             alpha * inv_sqrt_mass * inv_sqrt_mass,
             alpha * shift,
             beta * inv_sqrt_mass,
@@ -371,28 +569,11 @@
             -gamma * inverse,
             zero,
             zero,
-            zero,
         ]
     )
-    coef = lax.dynamic_slice_in_dim(coef, core * mine, mine, 1)
-    coef = jnp.concatenate([coef, lax.ppermute(coef[:, :RIM], BOTH, downs)], axis=1)
-
-    scaled = inv_sqrt_mass[None, :] * block
-    away = lax.dynamic_slice_in_dim(scaled, (1 - core) * mine, mine, 1)
-    kept = lax.dynamic_slice_in_dim(scaled, core * mine, mine, 1)
-    came = lax.ppermute(away, "grid", [(g, g ^ 1) for g in range(columns)])
-    field = jnp.where(
-        core == 0,
-        jnp.concatenate([kept, came], axis=0),
-        jnp.concatenate([came, kept], axis=0),
-    ).T
-    one = jnp.concatenate([field, lax.ppermute(field[:RIM], BOTH, downs)], axis=0)
-
+    one, coef = spread(parts, columns, block, coef)
     sums = element_sums(one, index, scale, matrix)
-    lower = lax.ppermute(sums[mine:], BOTH, ups)
-    upper = lax.ppermute(sums[:RIM], BOTH, downs)
-    assembled = jnp.concatenate([sums[:RIM] + lower, sums[RIM:mine], sums[mine:] + upper], axis=0)
-    two = coef[0][:, None] * assembled + coef[1][:, None] * one
+    two = middle(parts, columns, sums, one, coef)
     sums = element_sums(two, index, scale, matrix)
     return finish(parts, columns, states, owned, sums, one, two, coef)
 

time: 199 us -> 169 us (0.85)
  starting transfers between devices: 16.6 us -> 0 us
  other arithmetic: 15.7 us -> 1.55 us
  Pallas kernels: 146 us -> 160 us
  local copies, waits for them, and re-layouts: 14.6 us -> 6.44 us
  waiting for transfers between devices: 5.29 us -> 0 us
    pallas_call x0 -> x2, Pallas kernels: none -> 23.3 us  [the longest x1 12.5 us: middle(): pl.pallas_call(functools.partial(middle_kernel, parts, columns), out_shap...]
    ppermute x5 -> x0, starting transfers between devices: 16.6 us -> none  [the longest x1 12.1 us: shards(): lower = lax.ppermute(sums[mine:], BOTH, ups)]
    pallas_call x2, Pallas kernels: 40.7 us -> 35 us  [element_sums(): pl.pallas_call(functools.partial(operator_kernel, npe), out_shape=jax.Sha...]
    ppermute x5 -> x0, waiting for transfers between devices: 5.29 us -> none  [the longest x1 2.35 us: shards(): upper = lax.ppermute(sums[:RIM], BOTH, downs)]
    mul x1 -> x0, other arithmetic: 4.96 us -> none  [shards(): scaled = inv_sqrt_mass[None, :] * block]
    transpose x1 -> x0, other arithmetic: 4.73 us -> none  [shards(): field = jnp.where(core == 0, jnp.concatenate([kept, came], axis=0), jnp.c...]
    add x2 -> x0, other arithmetic: 4.37 us -> none  [the longest x1 4.1 us: shards(): two = coef[0][:, None] * assembled + coef[1][:, None] * one]
    pallas_call x1, Pallas kernels: 105 us -> 101 us  [finish(): pl.pallas_call(functools.partial(finish_kernel, parts, columns, pieces, 1...]
  transfers between devices with their start and end apart: 5 -> 0, of which waited for: 3 -> 0; matrix products, arithmetic and copies ran while one was open for 3% -> 0% of each run, Pallas kernels for 10% -> 0%
where the time goes in v3:
time: 169 us; the launch traced here: 168 us
  Pallas kernels  160 us (95%)
  local copies, waits for them, and re-layouts  6.44 us (4%)
    pallas_call x1, Pallas kernels, finish(): pl.pallas_call(functools.partial(finish_kernel, parts, columns, pieces, 1...  101 us
    pallas_call x2, Pallas kernels, element_sums(): pl.pallas_call(functools.partial(operator_kernel, npe), out_shape=jax.Sha...  35 us
    pallas_call x1, Pallas kernels, middle(): pl.pallas_call(functools.partial(middle_kernel, parts, columns), out_shap...  12.5 us
    pallas_call x1, Pallas kernels, spread(): pl.pallas_call(functools.partial(spread_kernel, parts, columns), out_shap...  10.8 us

profile of v3, /device:TPU:0, one launch (start us, length us, event | category | flops | bytes accessed | tf_op | source)
XLA Modules:
  0.0 168.5 jit_solution(4797131672891401652)
XLA Ops:
  0.6 0.7 dynamic_slice.7.scale_ref
  1.4 0.8 dynamic-slice_subtract_fusion
  2.1 0.1 reshape.8.index_ref
  2.3 0.8 pad.4.matrix_ref
  3.1 0.8 broadcast_multiply_fusion
  4.0 1.1 stack.31.coef_ref
  5.0 0.0 copy-start.1
  5.0 1.6 copy-done.1
  6.6 10.8 %shard_map.77 = (f32[6144,128]{1,0:T(8,128)S(1)}, f32[8,6144]{1,0:T(8,128)S(1)}) custom-call(f32[64,8192]{1,0:T(8,128)S(1)} %copy-done.1, f32[8,8192]{1,0:T(8,128)S(1)} %stack.31.coef_ref), custom_call_target="tpu_custom_call" | custom-call | tf_op jit(solution)/shard_map/pallas_call | solution.py:452
  17.5 17.5 %shard_map.78.sums_ref = f32[6144,128]{1,0:T(8,128)S(1)} custom-call(s32[8000]{0:T(1024)S(1)} %reshape.8.index_ref, f32[64]{0:T(128)S(1)} %dynamic_slice.7.scale_ref, f32[128,128]{1,0:T(8,128)S(1)} %pad.4.matrix_ref, f32[6144,128]{1,0:T(8,128)S(1)} %get-tuple-element.4.wide_ref.one_ref), custom_call_target="tpu_custom_call" | custom-call | tf_op jit(solution)/shard_map/pallas_call | solution.py:69
  35.0 12.5 %shard_map.79.wide_ref.two_ref = f32[6144,128]{1,0:T(8,128)S(1)} custom-call(f32[6144,128]{1,0:T(8,128)S(1)} %shard_map.78.sums_ref, f32[6144,128]{1,0:T(8,128)S(1)} %get-tuple-element.4.wide_ref.one_ref, f32[8,6144]{1,0:T(8,128)S(1)} %get-tuple-element.5.coef_ref), custom_call_target="tpu_custom_call" | custom-call | tf_op jit(solution)/shard_map/pallas_call | solution.py:529
  47.5 0.0 copy-start
  47.5 17.5 %shard_map.80.sums_ref = f32[6144,128]{1,0:T(8,128)S(1)} custom-call(s32[8000]{0:T(1024)S(1)} %reshape.8.index_ref, f32[64]{0:T(128)S(1)} %dynamic_slice.7.scale_ref, f32[128,128]{1,0:T(8,128)S(1)} %pad.4.matrix_ref, f32[6144,128]{1,0:T(8,128)S(1)} %shard_map.79.wide_ref.two_ref), custom_call_target="tpu_custom_call" | custom-call | tf_op jit(solution)/shard_map/pallas_call | solution.py:69
  65.0 0.0 copy-done
  65.0 101.4 %shard_map.81 = (f32[64,8192]{1,0:T(8,128)S(1)}, f32[256,64]{1,0:T(8,128)S(1)}) custom-call(f32[6144,128]{1,0:T(8,128)S(1)} %shard_map.80.sums_ref, f32[6144,128]{1,0:T(8,128)S(1)} %get-tuple-element.4.wide_ref.one_ref, f32[6144,128]{1,0:T(8,128)} %copy-done, f32[8,6144]{1,0:T(8,128)S(1)} %get-tuple-element.5.coef_ref), custom_call_target="tpu_custom_call" | custom-call | tf_op jit(solution)/shard_map/pallas_call | solution.py:301
  166.4 0.7 copy.8
  167.1 1.3 copy.10
  (1 shorter events, 0.0 us)
Async XLA Ops:
  5.0 1.6 copy-start.1
  47.5 17.5 %copy-start = (f32[6144,128]{1,0:T(8,128)}, f32[6144,128]{1,0:T(8,128)S(1)}, u32[]{:S(2)}) copy-start(f32[6144,128]{1,0:T(8,128)S(1)} %shard_map.79.wide_ref.two_ref) | copy-start | bytes 9437188

commit v4 on v3

--- a/solution.py
+++ b/solution.py
@@ -23,7 +23,10 @@
     return jnp.dot(a, b, preferred_element_type=jnp.float32)
 
 
-def operator_kernel(npe, index_ref, scale_ref, matrix_ref, wide_ref, out_ref, picked, local, *sums):
+def operator_kernel(
+    npe, base, index_ref, scale_ref, matrix_ref, all_ref, near_ref, far_ref, picked, local, *sums
+):
+    wide_ref = all_ref.at[pl.ds(base, 2 * RIM)]
     groups = scale_ref.shape[0] // GROUP
     m_high, m_low = split(matrix_ref[...])
     picked[...] = jnp.zeros_like(picked)
@@ -55,26 +58,42 @@
                 total[pl.ds(node, 1), :] += local[i : i + 1, m * 128 : (m + 1) * 128]
                 gather(later, i, m)
 
-    value = sums[0][...]
-    for total in sums[1:]:
-        value = value + total[...]
-    out_ref[...] = value
-
-
-def element_sums(wide, index, scale, matrix):
+    for target, start in ((near_ref, 0), (far_ref, RIM)):
+        value = sums[0][start : start + RIM, :]
+        for total in sums[1:]:
+            value = value + total[start : start + RIM, :]
+        target[...] = value
+
+
+def element_sums(wide, base, index, scale, matrix):
     count, npe = index.shape
+    piece = jax.ShapeDtypeStruct((RIM, wide.shape[1]), jnp.float32)
     vmem = pl.BlockSpec(memory_space=pltpu.VMEM)
     smem = pl.BlockSpec(memory_space=pltpu.SMEM)
     rows = matrix.shape[0]
     return pl.pallas_call(
-        functools.partial(operator_kernel, npe),
-        out_shape=jax.ShapeDtypeStruct(wide.shape, jnp.float32),
+        functools.partial(operator_kernel, npe, base),
+        out_shape=(piece, piece),
         in_specs=[smem, smem, vmem, vmem],
-        out_specs=vmem,
+        out_specs=(vmem, vmem),
         scratch_shapes=[pltpu.VMEM((rows, GROUP * 128), jnp.float32)] * 2
-        + [pltpu.VMEM(wide.shape, jnp.float32)] * CHAINS,
+        + [pltpu.VMEM((2 * RIM, wide.shape[1]), jnp.float32)] * CHAINS,
         compiler_params=pltpu.CompilerParams(vmem_limit_bytes=44 * 1024 * 1024),
-    )(index.reshape(-1), scale, matrix, wide)
+        cost_estimate=pl.CostEstimate(
+            flops=6 * count * rows * rows * wide.shape[1],
+            bytes_accessed=4 * (wide.size + 2 * piece.size + 8 * count * npe * wide.shape[1]),
+            transcendentals=0,
+        ),
+    )((index - base).reshape(-1), scale, matrix, wide)
+
+
+def both_sums(wide, index, scale, matrix, ups):
+    half = index.shape[0] // 2
+    inner, rim = element_sums(wide, RIM, index[half:], scale[half:], matrix)
+    lower = lax.ppermute(rim, BOTH, ups)
+    wide, rim = lax.optimization_barrier((wide, rim))
+    near, far = element_sums(wide, 0, index[:half], scale[:half], matrix)
+    return near, far, inner, rim, lower
 
 
 STRIDE = 11
@@ -93,15 +112,14 @@
 
 def finish_kernel(
     parts, columns, pieces, weight,
-    sums_ref, one_ref, two_ref, coef_ref, out_ref, panel_ref,
-    flat, send, rim, raw, high, low, gram, collected, stage, panel,
-    rim_sem, swap_sem, move_send, move_recv, part_send, part_recv, row_send, row_recv, own_sem,
+    near_ref, far_ref, inner_ref, lower_ref, one_ref, two_ref, coef_ref, out_ref, panel_ref,
+    flat, send, raw, high, low, gram, collected, stage, panel,
+    swap_sem, move_send, move_recv, part_send, part_recv, row_send, row_recv, own_sem,
 ):
     p, g = lax.axis_index("nodes"), lax.axis_index("grid")
     y, k = g // 2, lax.rem(g, 2)
     count = parts * columns
     me = p * columns + g
-    t, last = 2 * p + k, 2 * parts - 1
     mine = flat.shape[1]
     quarter = mine // 4
     width = mine // parts
@@ -120,22 +138,6 @@
     )
     pl.semaphore_wait(barrier, count - 1)
 
-    def rim_copy():
-        up = t + 1
-        return pltpu.make_async_remote_copy(
-            src_ref=sums_ref.at[pl.ds(mine, RIM)], dst_ref=rim,
-            send_sem=rim_sem.at[0], recv_sem=rim_sem.at[1],
-            device_id=(up // 2, 2 * y + lax.rem(up, 2)), device_id_type=MESH,
-        )
-
-    @pl.when(t < last)
-    def _():
-        rim_copy().start()
-
-    @pl.when(t == 0)
-    def _():
-        rim[...] = jnp.zeros_like(rim)
-
     def swap_copy(h):
         start = pl.multiple_of((2 * h + 1 - y) * quarter, 128)
         return pltpu.make_async_remote_copy(
@@ -161,9 +163,11 @@
     def combine(b, with_rim):
         at = pl.multiple_of(b * 128, 128)
         rows = pl.ds(at, 128)
-        value = sums_ref[rows, :]
         if with_rim:
-            value = value + rim[rows, :]
+            value = near_ref[rows, :] + lower_ref[rows, :]
+        else:
+            behind = pl.ds(pl.multiple_of(at - RIM, 128), 128)
+            value = far_ref[behind, :] + inner_ref[behind, :]
         result = (
             value.T * coef_ref[3:4, rows]
             + two_ref[rows, :].T * coef_ref[4:5, rows]
@@ -191,10 +195,6 @@
     if pieces == 2:
         others(count, me, lambda d: move(d, 1, me).start())
     keep(1)
-
-    @pl.when(t > 0)
-    def _():
-        rim_copy().wait_recv()
 
     @pl.loop(0, half)
     def _(b):
@@ -284,12 +284,8 @@
     others(count, me, lambda d: if_owner(d, lambda: part(d, me).wait_send()))
     if_owner(me, lambda: others(count, me, lambda d: row(d, me).wait_send()))
 
-    @pl.when(t < last)
-    def _():
-        rim_copy().wait_send()
-
-
-def finish(parts, columns, states, owned, sums, one, two, coef):
+
+def finish(parts, columns, states, owned, near, far, inner, lower, one, two, coef):
     mine = owned // 2
     count = parts * columns
     width = mine // parts
@@ -304,12 +300,11 @@
             jax.ShapeDtypeStruct((states, owned), f32),
             jax.ShapeDtypeStruct((total, states), f32),
         ),
-        in_specs=[vmem] * 4,
+        in_specs=[vmem] * 7,
         out_specs=(pl.BlockSpec(memory_space=pl.ANY), vmem),
         scratch_shapes=[
             pltpu.VMEM((2 * states, mine), f32),
             pltpu.VMEM((count, 2 * SB, width), f32),
-            pltpu.VMEM((RIM, 2 * states), f32),
             pltpu.VMEM((2, total, mine // 4), f32),
             pltpu.VMEM((total, mine // 4), bf16),
             pltpu.VMEM((total, mine // 4), bf16),
@@ -317,13 +312,13 @@
             pltpu.VMEM((count, 8, total), f32),
             pltpu.VMEM((columns, 8, 128), f32),
             pltpu.VMEM((total, 128), f32),
-            dma((2,)), dma((2, 2)), dma((pieces, count)), dma((pieces, count)),
+            dma((2, 2)), dma((pieces, count)), dma((pieces, count)),
             dma((count,)), dma((count,)), dma((count,)), dma((count,)), dma((pieces,)),
         ],
         compiler_params=pltpu.CompilerParams(
             collective_id=0, has_side_effects=True, vmem_limit_bytes=44 * 1024 * 1024
         ),
-    )(sums, one, two, coef)
+    )(near, far, inner, lower, one, two, coef)
 
 
 def seat(columns):
@@ -469,10 +464,11 @@
     )(block, coef)
 
 
-def middle_kernel(parts, columns, sums_ref, one_ref, coef_ref, two_ref, lower, upper, sems):
+def middle_kernel(
+    parts, columns, near_ref, far_ref, inner_ref, rim_ref, lower_ref, one_ref, coef_ref, two_ref, upper, sems
+):
     p, g, y, k = seat(columns)
     t, last = 2 * p + k, 2 * parts - 1
-    mine = sums_ref.shape[0] - RIM
 
     def device(t):
         return (t // 2, 2 * y + lax.rem(t, 2))
@@ -487,55 +483,45 @@
         )
     pl.semaphore_wait(barrier, jnp.where(has_up, 1, 0) + jnp.where(has_down, 1, 0))
 
-    def rise():
-        return remote(sums_ref.at[pl.ds(mine, RIM)], lower, sems, 0, device(t + 1))
-
     def fall():
-        return remote(sums_ref.at[pl.ds(0, RIM)], upper, sems, 1, device(t - 1))
-
-    pl.when(has_up)(lambda: rise().start())
+        return remote(near_ref, upper, sems, 0, device(t - 1))
+
     pl.when(has_down)(lambda: fall().start())
 
-    @pl.when(t == 0)
-    def _():
-        lower[...] = jnp.zeros_like(lower)
-
     @pl.when(t == last)
     def _():
         upper[...] = jnp.zeros_like(upper)
 
-    def combine(b, extra, base):
-        rows = pl.ds(pl.multiple_of(b * 128, 128), 128)
-        value = sums_ref[rows, :]
-        if extra is not None:
-            value = value + extra[pl.ds(pl.multiple_of((b - base) * 128, 128), 128), :]
-        size = (128, 128)
-        one = jnp.broadcast_to(coef_ref[1:2, rows], size).T
-        two = jnp.broadcast_to(coef_ref[2:3, rows], size).T
-        two_ref[rows, :] = one * value + two * one_ref[rows, :]
-
-    pl.loop(RIM // 128, mine // 128)(lambda b: combine(b, None, 0))
-    pl.when(has_down)(lambda: rise().wait_recv())
-    pl.loop(0, RIM // 128)(lambda b: combine(b, lower, 0))
+    def combine(base, a_ref, b_ref):
+        @pl.loop(0, RIM // 128)
+        def _(b):
+            here = pl.ds(pl.multiple_of(b * 128, 128), 128)
+            rows = pl.ds(pl.multiple_of(base + b * 128, 128), 128)
+            size = (128, 128)
+            one = jnp.broadcast_to(coef_ref[1:2, rows], size).T
+            two = jnp.broadcast_to(coef_ref[2:3, rows], size).T
+            value = a_ref[here, :] + b_ref[here, :]
+            two_ref[rows, :] = one * value + two * one_ref[rows, :]
+
+    combine(0, near_ref, lower_ref)
+    combine(RIM, far_ref, inner_ref)
     pl.when(has_up)(lambda: fall().wait_recv())
-    pl.loop(mine // 128, (mine + RIM) // 128)(lambda b: combine(b, upper, mine // 128))
-    pl.when(has_up)(lambda: rise().wait_send())
+    combine(2 * RIM, rim_ref, upper)
     pl.when(has_down)(lambda: fall().wait_send())
 
 
-def middle(parts, columns, sums, one, coef):
+def middle(parts, columns, near, far, inner, rim, lower, one, coef):
     vmem = pl.BlockSpec(memory_space=pltpu.VMEM)
-    rim = pltpu.VMEM((RIM, sums.shape[1]), jnp.float32)
     return pl.pallas_call(
         functools.partial(middle_kernel, parts, columns),
-        out_shape=jax.ShapeDtypeStruct(sums.shape, jnp.float32),
-        in_specs=[vmem] * 3,
+        out_shape=jax.ShapeDtypeStruct(one.shape, jnp.float32),
+        in_specs=[vmem] * 7,
         out_specs=vmem,
-        scratch_shapes=[rim, rim, pltpu.SemaphoreType.DMA((2, 2))],
+        scratch_shapes=[pltpu.VMEM(near.shape, jnp.float32), pltpu.SemaphoreType.DMA((2, 1))],
         compiler_params=pltpu.CompilerParams(
             collective_id=2, has_side_effects=True, vmem_limit_bytes=44 * 1024 * 1024
         ),
-    )(sums, one, coef)
+    )(near, far, inner, rim, lower, one, coef)
 
 
 def shards(block, inv_sqrt_mass, potential, elem_scale, connectivity, elem_matrix):
@@ -572,10 +558,15 @@
         ]
     )
     one, coef = spread(parts, columns, block, coef)
-    sums = element_sums(one, index, scale, matrix)
-    two = middle(parts, columns, sums, one, coef)
-    sums = element_sums(two, index, scale, matrix)
-    return finish(parts, columns, states, owned, sums, one, two, coef)
+    ups = []
+    for y in range(columns // 2):
+        for t in range(2 * parts - 1):
+            below = (t // 2) * columns + 2 * y + t % 2
+            ups.append((below, ((t + 1) // 2) * columns + 2 * y + (t + 1) % 2))
+    near, far, inner, rim, lower = both_sums(one, index, scale, matrix, ups)
+    two = middle(parts, columns, near, far, inner, rim, lower, one, coef)
+    near, far, inner, rim, lower = both_sums(two, index, scale, matrix, ups)
+    return finish(parts, columns, states, owned, near, far, inner, lower, one, two, coef)
 
 
 def solution(mesh):

time: 169 us -> 177 us (1.047)
  starting transfers between devices: 0 us -> 23 us
  Pallas kernels: 160 us -> 143 us
  local copies, waits for them, and re-layouts: 6.44 us -> 8.29 us
    ppermute x0 -> x2, starting transfers between devices: none -> 23 us  [both_sums(): lower = lax.ppermute(rim, BOTH, ups)]
    pallas_call x1, Pallas kernels: 101 us -> 82.8 us  [finish(): pl.pallas_call(functools.partial(finish_kernel, parts, columns, pieces, 1...]
    pallas_call x2 -> x4, Pallas kernels: 35 us -> 39.1 us  [element_sums(): pl.pallas_call(functools.partial(operator_kernel, npe, base), out_shape=(...]
    pallas_call x1, Pallas kernels: 12.5 us -> 10.2 us  [middle(): pl.pallas_call(functools.partial(middle_kernel, parts, columns), out_shap...]
    unnamed x5 -> x17, local copies, waits for them, and re-layouts: 2.91 us -> 4.62 us
  transfers between devices with their start and end apart: 0 -> 2, of which waited for: 0 -> 0; matrix products, arithmetic and copies ran while one was open for 0% -> 0% of each run, Pallas kernels for 0% -> 11%
where the time goes in v4:
time: 177 us
  Pallas kernels  143 us (81%)
  starting transfers between devices  23 us (13%)
  local copies, waits for them, and re-layouts  8.29 us (5%)
    pallas_call x1, Pallas kernels, finish(): pl.pallas_call(functools.partial(finish_kernel, parts, columns, pieces, 1...  82.8 us
    pallas_call x4, Pallas kernels, element_sums(): pl.pallas_call(functools.partial(operator_kernel, npe, base), out_shape=(...  39.1 us
    ppermute x2, starting transfers between devices, both_sums(): lower = lax.ppermute(rim, BOTH, ups)  23 us
    pallas_call x1, Pallas kernels, spread(): pl.pallas_call(functools.partial(spread_kernel, parts, columns), out_shap...  10.8 us
    pallas_call x1, Pallas kernels, middle(): pl.pallas_call(functools.partial(middle_kernel, parts, columns), out_shap...  10.2 us
    unnamed x17, local copies, waits for them, and re-layouts  4.62 us
  transfers between devices with their start and end apart: 2, of which 0 were waited for; matrix products, arithmetic and copies ran while one was open for 0% of the time, Pallas kernels for 11%

profile of v4, /device:TPU:0, one launch (start us, length us, event | category | flops | bytes accessed | tf_op | source)
XLA Modules:
  0.0 176.6 jit_solution(11383512747710081710)
XLA Ops:
  0.6 0.7 dynamic_slice.7
  1.4 0.1 fusion
  1.5 0.8 dynamic-slice_subtract_fusion
  2.2 0.1 reshape.13.index_ref
  2.3 0.8 pad.4.matrix_ref
  3.2 0.8 broadcast_multiply_fusion
  4.0 1.1 stack.31.coef_ref
  5.1 0.0 copy-start.3
  5.1 1.6 copy-done.3
  6.7 10.8 %shard_map.77 = (f32[6144,128]{1,0:T(8,128)S(1)}, f32[8,6144]{1,0:T(8,128)S(1)}) custom-call(f32[64,8192]{1,0:T(8,128)S(1)} %copy-done.3, f32[8,8192]{1,0:T(8,128)S(1)} %stack.31.coef_ref), custom_call_target="tpu_custom_call" | custom-call | tf_op jit(solution)/shard_map/pallas_call | solution.py:447
  17.5 0.0 copy-start.6
  17.5 0.7 copy-done.6
  18.2 0.0 copy-start
  18.2 10.2 %shard_map.78 = (f32[2048,128]{1,0:T(8,128)S(1)}, f32[2048,128]{1,0:T(8,128)}) custom-call(s32[4000]{0:T(1024)S(1)} %reshape.13.index_ref, f32[32]{0:T(128)S(1)} %get-tuple-element.37.scale_ref, f32[128,128]{1,0:T(8,128)S(1)} %pad.4.matrix_ref, f32[6144,128]{1,0:T(8,128)S(1)} %get-tuple-element.17.all_ref.one_ref), custom_call_target="tpu_custom_call" | custom-call | flops 402653184 | bytes 21626880 | tf_op jit(solution)/shard_map/pallas_call | solution.py:74
  28.5 0.0 copy-start.4
  28.5 1.0 copy-done.4
  29.5 0.0 copy-start.7
  29.5 10.3 %collective-permute-start = (f32[2048,128]{1,0:T(8,128)}, f32[2048,128]{1,0:T(8,128)}, u32[]{:S(2)}, u32[]{:S(2)}) collective-permute-start(f32[2048,128]{1,0:T(8,128)} %get-tuple-element.21.rim_ref), channel_id=1, source_target_pairs={{0,1},{1,4},{4,5},{5,8},{8,9},{9,12},{12,13},{13,16},{16,17},{17,2... | collective-permute-start | bytes 3145736 | tf_op jit(solution)/shard_map/ppermute | solution.py:93
  39.8 0.1 reshape.12.index_ref
  39.9 0.0 copy-start.5
  39.9 9.6 %shard_map.79 = (f32[2048,128]{1,0:T(8,128)S(1)}, f32[2048,128]{1,0:T(8,128)S(1)}) custom-call(s32[4000]{0:T(1024)S(1)} %reshape.12.index_ref, f32[32]{0:T(128)S(1)} %get-tuple-element.38.scale_ref, f32[128,128]{1,0:T(8,128)S(1)} %pad.4.matrix_ref, f32[6144,128]{1,0:T(8,128)S(1)} %get-tuple-element.17.all_ref.one_ref), custom_call_target="tpu_custom_call" | custom-call | flops 402653184 | bytes 21626880 | tf_op jit(solution)/shard_map/pallas_call | solution.py:74
  49.5 0.0 copy-done
  49.5 0.0 collective-permute-done.lower_ref
  49.5 0.0 copy-done.7
  49.5 0.0 copy-done.5
  49.6 10.2 %shard_map.80.all_ref.two_ref = f32[6144,128]{1,0:T(8,128)S(1)} custom-call(f32[2048,128]{1,0:T(8,128)S(1)} %get-tuple-element.18.near_ref, f32[2048,128]{1,0:T(8,128)S(1)} %get-tuple-element.19.far_ref, f32[2048,128]{1,0:T(8,128)S(1)} %copy-done.5, f32[2048,128]{1,0:T(8,128)} %get-tuple-element.21.rim_ref, f32[2048,128]{1,0:T(8,128)} %collective-permute-done.lower_ref, ...), custom_call_target="tpu_custom_call" | custom-call | tf_op jit(solution)/shard_map/pallas_call | solution.py:515
  59.7 0.0 copy-start.2
  59.7 9.6 %shard_map.81 = (f32[2048,128]{1,0:T(8,128)S(1)}, f32[2048,128]{1,0:T(8,128)S(1)}) custom-call(s32[4000]{0:T(1024)S(1)} %reshape.13.index_ref, f32[32]{0:T(128)S(1)} %get-tuple-element.37.scale_ref, f32[128,128]{1,0:T(8,128)S(1)} %pad.4.matrix_ref, f32[6144,128]{1,0:T(8,128)S(1)} %shard_map.80.all_ref.two_ref), custom_call_target="tpu_custom_call" | custom-call | flops 402653184 | bytes 21626880 | tf_op jit(solution)/shard_map/pallas_call | solution.py:74
  69.3 0.0 copy-start.1
  69.3 12.7 %collective-permute-start.1 = (f32[2048,128]{1,0:T(8,128)S(1)}, f32[2048,128]{1,0:T(8,128)S(1)}, u32[]{:S(2)}, u32[]{:S(2)}) collective-permute-start(f32[2048,128]{1,0:T(8,128)S(1)} %get-tuple-element.23), channel_id=1, source_target_pairs={{0,1},{1,4},{4,5},{5,8},{8,9},{9,12},{12,13},{13,16},{16,17},{17,2... | collective-permute-start | bytes 3145736 | tf_op jit(solution)/shard_map/ppermute | solution.py:93
  82.1 9.6 %shard_map.82 = (f32[2048,128]{1,0:T(8,128)S(1)}, f32[2048,128]{1,0:T(8,128)S(1)}) custom-call(s32[4000]{0:T(1024)S(1)} %reshape.12.index_ref, f32[32]{0:T(128)S(1)} %get-tuple-element.38.scale_ref, f32[128,128]{1,0:T(8,128)S(1)} %pad.4.matrix_ref, f32[6144,128]{1,0:T(8,128)S(1)} %shard_map.80.all_ref.two_ref), custom_call_target="tpu_custom_call" | custom-call | flops 402653184 | bytes 21626880 | tf_op jit(solution)/shard_map/pallas_call | solution.py:74
  91.7 0.0 copy-done.2
  91.7 0.0 collective-permute-done.1.lower_ref
  91.7 0.0 copy-done.1
  91.8 82.8 %shard_map.83 = (f32[64,8192]{1,0:T(8,128)S(1)}, f32[256,64]{1,0:T(8,128)S(1)}) custom-call(f32[2048,128]{1,0:T(8,128)S(1)} %get-tuple-element.25.near_ref, f32[2048,128]{1,0:T(8,128)S(1)} %get-tuple-element.26.far_ref, f32[2048,128]{1,0:T(8,128)S(1)} %get-tuple-element.27.inner_ref, f32[2048,128]{1,0:T(8,128)S(1)} %collective-permute-done.1.lower_ref, ...), custom_call_target="tpu_custom_call" | custom-call | tf_op jit(solution)/shard_map/pallas_call | solution.py:297
  174.6 0.7 copy.8
  175.3 1.3 copy.10
  (2 shorter events, 0.0 us)
Async XLA Ops:
  5.1 1.6 copy-start.3
  17.5 0.7 copy-start.6
  18.2 31.3 %copy-start = (f32[6144,128]{1,0:T(8,128)}, f32[6144,128]{1,0:T(8,128)S(1)}, u32[]{:S(2)}) copy-start(f32[6144,128]{1,0:T(8,128)S(1)} %get-tuple-element.17.all_ref.one_ref) | copy-start | bytes 9437188
  28.5 1.0 copy-start.4
  29.5 20.1 %copy-start.7 = (f32[8,6144]{1,0:T(8,128)S(1)}, f32[8,6144]{1,0:T(8,128)}, u32[]{:S(2)}) copy-start(f32[8,6144]{1,0:T(8,128)} %copy-done.6) | copy-start | bytes 589828
  29.5 20.0 %collective-permute-start = (f32[2048,128]{1,0:T(8,128)}, f32[2048,128]{1,0:T(8,128)}, u32[]{:S(2)}, u32[]{:S(2)}) collective-permute-start(f32[2048,128]{1,0:T(8,128)} %get-tuple-element.21.rim_ref), channel_id=1, source_target_pairs={{0,1},{1,4},{4,5},{5,8},{8,9},{9,12},{12,13},{13,16},{16,17},{17,2... | collective-permute-start | bytes 3145736 | tf_op jit(solution)/shard_map/ppermute | solution.py:93
  39.9 9.7 %copy-start.5 = (f32[2048,128]{1,0:T(8,128)S(1)}, f32[2048,128]{1,0:T(8,128)}, u32[]{:S(2)}) copy-start(f32[2048,128]{1,0:T(8,128)} %copy-done.4) | copy-start | bytes 3145732
  59.7 32.0 %copy-start.2 = (f32[6144,128]{1,0:T(8,128)}, f32[6144,128]{1,0:T(8,128)S(1)}, u32[]{:S(2)}) copy-start(f32[6144,128]{1,0:T(8,128)S(1)} %shard_map.80.all_ref.two_ref) | copy-start | bytes 9437188
  69.3 22.4 %copy-start.1 = (f32[6144,128]{1,0:T(8,128)S(1)}, f32[6144,128]{1,0:T(8,128)}, u32[]{:S(2)}) copy-start(f32[6144,128]{1,0:T(8,128)} %copy-done) | copy-start | bytes 9437188
  69.3 22.4 %collective-permute-start.1 = (f32[2048,128]{1,0:T(8,128)S(1)}, f32[2048,128]{1,0:T(8,128)S(1)}, u32[]{:S(2)}, u32[]{:S(2)}) collective-permute-start(f32[2048,128]{1,0:T(8,128)S(1)} %get-tuple-element.23), channel_id=1, source_target_pairs={{0,1},{1,4},{4,5},{5,8},{8,9},{9,12},{12,13},{13,16},{16,17},{17,2... | collective-permute-start | bytes 3145736 | tf_op jit(solution)/shard_map/ppermute | solution.py:93
